TPU v7x, 128 devices: a whole 4x4x4 slice. The times are simulated.
128 devices in a mesh: dp: 4 (over x), expert: 16 (over y, z), blk: 2 (over core).
Axes of the slice: x: 4, y: 4, z: 4, core: 2. Of those that a mesh axis runs over, the one named last changes fastest.
Arguments:
- tokens_in: bfloat16 [8192, 1536], P(('dp', 'expert'), 'blk'), may hold values from -6 to 6
- seq_lengths: int32 [64, 3], P(('dp', 'expert')), may hold values from 1 to 64, 128 in all within a row
- expert_ids: int32 [2, 8192, 4], P(None, ('dp', 'expert')), may hold values from 0 to 31, all different within a row; in each aligned block of 128 rows (0 to 127, 128 to 255, ..., all dimensions but the last counted through in order) at most 24 rows name the same one
- gate_weights: float32 [2, 8192, 4], P(None, ('dp', 'expert')), may hold values from 0.12 to 0.48
- attention_gain: bfloat16 [2, 1536], P(None, ('dp', 'expert')), may hold values from 0.099609375 to 1.8984375
- query_weight: bfloat16 [2, 1536, 1536], P(None, ('dp', 'expert'), 'blk'), may hold values from -0.15625 to 0.15625
- key_weight: bfloat16 [2, 1536, 256], P(None, ('dp', 'expert'), 'blk'), may hold values from -0.15625 to 0.15625
- value_weight: bfloat16 [2, 1536, 256], P(None, ('dp', 'expert'), 'blk'), may hold values from -0.15625 to 0.15625
- out_weight: bfloat16 [2, 1536, 1536], P(None, 'blk', ('dp', 'expert')), may hold values from -0.625 to 0.625
- expert_gain: bfloat16 [2, 1536], P(None, ('dp', 'expert')), may hold values from 0.099609375 to 1.8984375
- gate_weight: bfloat16 [2, 32, 1536, 768], P(None, 'expert', None, 'blk'), may hold values from -0.15625 to 0.15625
- up_weight: bfloat16 [2, 32, 1536, 768], P(None, 'expert', None, 'blk'), may hold values from -0.15625 to 0.15625
- down_weight: bfloat16 [2, 32, 768, 1536], P(None, 'expert', 'blk'), may hold values from -0.4375 to 0.4375
- cotangent: bfloat16 [8192, 1536], P(('dp', 'expert'), 'blk'), may hold values from -6 to 6
Outputs:
- block_out: bfloat16 [8192, 1536], P(('dp', 'expert'), 'blk')
- grad_tokens: float32 [8192, 1536], P(('dp', 'expert'), 'blk')
- grad_attention_gain: float32 [2, 1536], P(None, ('dp', 'expert'))
- grad_query_weight: float32 [2, 1536, 1536], P(None, ('dp', 'expert'), 'blk')
- grad_key_weight: float32 [2, 1536, 256], P(None, ('dp', 'expert'), 'blk')
- grad_value_weight: float32 [2, 1536, 256], P(None, ('dp', 'expert'), 'blk')
- grad_out_weight: float32 [2, 1536, 1536], P(None, 'blk', ('dp', 'expert'))
- grad_expert_gain: float32 [2, 1536], P(None, ('dp', 'expert'))
- grad_gate_weight: float32 [2, 32, 1536, 768], P(None, 'expert', 'dp', 'blk')
- grad_up_weight: float32 [2, 32, 1536, 768], P(None, 'expert', 'dp', 'blk')
- grad_down_weight: float32 [2, 32, 768, 1536], P(None, 'expert', 'blk', 'dp')
Inputs may be any that keep to these rules, and one draw needn't show every extreme that they name: `seq_lengths`: each row holds one group's 3 sequence lengths, which sum to 128; the longest is exactly 64. `expert_ids`: a token's 4 ids in a layer differ; in one layer, among the 128 tokens of one group (the rows of one device), no expert is named more than 24 times, a bound that some block reaches.
All inputs are finite; a program needn't handle non-finite values.
Results may differ from a plain program's by a relative error of at most 0.025.
Values may be sent and summed in bfloat16 or wider, within the bound.
A program may use at most 256 MiB of HBM per device.

v0:
```python
import jax
import jax.numpy as jnp
from jax import lax
from jax.sharding import PartitionSpec as P

HEAD = 128
TOP = 4
LAYERS = 2


epsilon = 1e-06
rope_base = 1000000.0


def total_of_pieces(value, axis):
    blocks = lax.all_gather(value, axis)
    return blocks.sum(axis=0)


def joined_along(blocks, dim):
    blocks = jnp.moveaxis(blocks, 0, dim)
    lengths = blocks.shape
    return blocks.reshape(*lengths[:dim], lengths[dim] * lengths[dim + 1], *lengths[dim + 2 :])


def copy_for_each(value, axis):
    copies = jnp.broadcast_to(value, (lax.axis_size(axis), *value.shape))
    return lax.all_to_all(copies, axis, split_axis=0, concat_axis=0, tiled=True)


def gather_directly(value, axis, dim):
    return joined_along(copy_for_each(value, axis), dim)


def split_up(value, dim, devices):
    lengths = value.shape
    blocks = value.reshape(*lengths[:dim], devices, lengths[dim] // devices, *lengths[dim + 1 :])
    return jnp.moveaxis(blocks, dim, 0)


def summed_on_arrival(value, axis, dim):
    blocks = split_up(value, dim, lax.axis_size(axis))
    arrived = lax.all_to_all(blocks, axis, split_axis=0, concat_axis=0, tiled=True)
    return arrived.astype(jnp.float32).sum(axis=0)


def gather_turned(arrays, axis, dims):
    turned = [jnp.moveaxis(a, dim, 0) for a, dim in zip(arrays, dims)]
    both = jnp.concatenate([t.reshape(len(t), -1) for t in turned], axis=1)
    whole, at, gathered = (lax.all_gather(both, axis, axis=0, tiled=True), 0, [])
    for t, dim in zip(turned, dims):
        share = whole[:, at : at + t[0].size].reshape(-1, *t.shape[1:])
        gathered.append(jnp.moveaxis(share, 0, dim))
        at += t[0].size
    return tuple(gathered)


def sent_together(arrays, axis, dim, along):
    columns = [a.reshape(*a.shape[:along], -1) for a in arrays]
    both = jnp.concatenate(columns, axis=along)
    whole, at, gathered = (lax.psum_scatter(both, axis, scatter_dimension=dim, tiled=True), 0, [])
    for a, column in zip(arrays, columns):
        share = whole[..., at : at + column.shape[along]]
        gathered.append(share.reshape(*share.shape[:along], *a.shape[along:]))
        at += column.shape[along]
    return tuple(gathered)


def in_one_piece(arrays, axis, dim, along):
    both = jnp.concatenate(arrays, axis=along)
    whole, at, gathered = (lax.psum_scatter(both, axis, scatter_dimension=dim, tiled=True), 0, [])
    for a in arrays:
        gathered.append(lax.slice_in_dim(whole, at, at + a.shape[along], axis=along))
        at += a.shape[along]
    return tuple(gathered)


def positions(lengths, row_count):
    seq_ends = jnp.cumsum(lengths)
    starts = seq_ends - lengths
    places = jnp.arange(row_count, dtype=jnp.int32)
    segment = jnp.sum((places[:, None] >= seq_ends[None, :]).astype(jnp.int32), axis=1)
    chosen = segment[:, None] == jnp.arange(lengths.shape[0], dtype=jnp.int32)[None, :]
    offset = jnp.sum(jnp.where(chosen, starts[None, :], 0), axis=1)
    return (segment, places - offset)


def rope_tables(places):
    half_dim = HEAD // 2
    frequency = rope_base ** (-2.0 * jnp.arange(half_dim, dtype=jnp.float32) / HEAD)
    angles = places.astype(jnp.float32)[:, None] * frequency[None, :]
    cosine_table = jnp.concatenate([jnp.cos(angles), jnp.cos(angles)], axis=-1)
    sine_table = jnp.concatenate([jnp.sin(angles), jnp.sin(angles)], axis=-1)
    return (cosine_table, sine_table)


def rotate(tensor, cosine_table, sine_table):
    half_dim = tensor.shape[-1] // 2
    turned = jnp.concatenate([-tensor[..., half_dim:], tensor[..., :half_dim]], axis=-1)
    return tensor * cosine_table + turned * sine_table


def unrotate(tensor, cosine_table, sine_table):
    half_dim = tensor.shape[-1] // 2
    weighted = tensor * sine_table
    turned = jnp.concatenate([weighted[..., half_dim:], -weighted[..., :half_dim]], axis=-1)
    return tensor * cosine_table + turned


def norm_forward(values_in, gain_vec):
    inverse = lax.rsqrt(jnp.mean(values_in * values_in, axis=-1, keepdims=True) + epsilon)
    return (values_in * inverse * gain_vec, inverse)


def norm_back(values_in, inverse, gain_vec, upstream):
    scaled = upstream * gain_vec
    inward = inverse * scaled - values_in * inverse**3 * jnp.mean(
        values_in * scaled, axis=-1, keepdims=True
    )
    return (inward, jnp.sum(upstream * values_in * inverse, axis=0))


def slot_numbers(expert_rows, experts, capacity):
    flattened = expert_rows.reshape(-1)
    onehot = (flattened[:, None] == jnp.arange(experts, dtype=jnp.int32)[None, :]).astype(jnp.int32)
    arrival = jnp.sum(jnp.cumsum(onehot, axis=0) * onehot, axis=1) - 1
    return flattened * capacity + arrival


def pair_total(partial_sum):
    return total_of_pieces(partial_sum, "blk")


def pair_grad(partial_sum):
    return total_of_pieces(partial_sum, "blk")


def widen_rows(half_rows):
    return gather_directly(half_rows, "blk", 3)


def split_pair(partial_sum):
    return summed_on_arrival(partial_sum.astype(jnp.bfloat16), "blk", 3)


def join_pair(half_rows):
    return gather_directly(half_rows, "blk", 1)


def per_device(
    tokens_in,
    seq_lengths,
    expert_ids,
    gate_weights,
    attention_gain,
    query_weight,
    key_weight,
    value_weight,
    out_weight,
    expert_gain,
    gate_weight,
    up_weight,
    down_weight,
    cotangent,
):
    blk_count = lax.axis_size("blk")
    blk_place = lax.axis_index("blk")
    expert_count = lax.axis_size("expert")
    stream = gather_directly(tokens_in, "blk", 1).astype(jnp.float32)
    group_rows, full_width = stream.shape
    half_width = full_width // blk_count
    experts = expert_count * gate_weight.shape[1]
    capacity = 3 * TOP * group_rows // (2 * experts)
    segment, places = positions(seq_lengths[0], group_rows)
    cosine_table, sine_table = rope_tables(places)
    allowed = (segment[:, None] == segment[None, :]) & (places[None, :] <= places[:, None])
    score_scale = HEAD ** (-0.5)
    kept_state = []
    for layer_index in range(LAYERS):
        query_full, key_full, value_full, out_full, gain_attention, gain_expert = gather_turned(
            (
                query_weight[layer_index],
                key_weight[layer_index],
                value_weight[layer_index],
                out_weight[layer_index],
                attention_gain[layer_index],
                expert_gain[layer_index],
            ),
            ("dp", "expert"),
            (0, 0, 0, 1, 0, 0),
        )
        stream_in = stream
        normed, inverse_attn = norm_forward(stream_in, gain_attention.astype(jnp.float32))
        normed = normed.astype(jnp.bfloat16)
        query_heads = jnp.dot(normed, query_full, preferred_element_type=jnp.float32)
        local_heads = query_heads.shape[1] // HEAD
        query_rot = rotate(
            query_heads.reshape(group_rows, local_heads, HEAD),
            cosine_table[:, None],
            sine_table[:, None],
        ).astype(jnp.bfloat16)
        key_heads = jnp.dot(normed, key_full, preferred_element_type=jnp.float32)
        kv_local = key_heads.shape[1] // HEAD
        key_rot = rotate(
            key_heads.reshape(group_rows, kv_local, HEAD),
            cosine_table[:, None],
            sine_table[:, None],
        ).astype(jnp.bfloat16)
        value_heads = (
            jnp.dot(normed, value_full, preferred_element_type=jnp.float32)
            .astype(jnp.bfloat16)
            .reshape(group_rows, kv_local, HEAD)
        )
        head_share = local_heads // kv_local
        query_group = query_rot.reshape(group_rows, kv_local, head_share, HEAD)
        raw_scores = (
            jnp.einsum("qhgd,khd->hgqk", query_group, key_rot, preferred_element_type=jnp.float32)
            * score_scale
        )
        masked = jnp.where(allowed, raw_scores, -1e30)
        top_score = jnp.max(masked, axis=-1, keepdims=True)
        log_total = top_score + jnp.log(
            jnp.sum(jnp.exp(masked - top_score), axis=-1, keepdims=True)
        )
        probability = jnp.exp(masked - log_total).astype(jnp.bfloat16)
        mixed_heads = (
            jnp.einsum(
                "hgqk,khd->qhgd", probability, value_heads, preferred_element_type=jnp.float32
            )
            .reshape(group_rows, local_heads * HEAD)
            .astype(jnp.bfloat16)
        )
        hidden = stream_in + pair_total(
            jnp.dot(mixed_heads, out_full, preferred_element_type=jnp.float32)
        )
        normed_exp, inverse_exp = norm_forward(hidden, gain_expert.astype(jnp.float32))
        normed_exp = normed_exp.astype(jnp.bfloat16)
        slot_index = slot_numbers(expert_ids[layer_index], experts, capacity)
        owners = jnp.arange(group_rows * TOP, dtype=jnp.int32) // TOP
        slot_owner = jnp.zeros((experts * capacity,), jnp.int32).at[slot_index].set(owners)
        slot_live = jnp.zeros((experts * capacity,), jnp.bool_).at[slot_index].set(True)
        slot_gate = (
            jnp.zeros((experts * capacity,), jnp.float32)
            .at[slot_index]
            .set(gate_weights[layer_index].reshape(-1))
        )
        outgoing = jnp.where(
            slot_live[:, None], normed_exp[slot_owner], jnp.zeros((), jnp.bfloat16)
        ).reshape(expert_count, -1, capacity, full_width)
        outgoing = lax.dynamic_slice_in_dim(outgoing, blk_place * half_width, half_width, 3)
        gate_local = gate_weight[layer_index]
        up_local = up_weight[layer_index]
        down_local = down_weight[layer_index]
        arrived_rows = lax.all_to_all(outgoing, "expert", split_axis=0, concat_axis=0, tiled=True)
        arrived_rows = widen_rows(arrived_rows)
        gate_act = jnp.einsum(
            "secd,edf->secf", arrived_rows, gate_local, preferred_element_type=jnp.float32
        )
        up_act = jnp.einsum(
            "secd,edf->secf", arrived_rows, up_local, preferred_element_type=jnp.float32
        )
        serve_inner_act = (jax.nn.silu(gate_act) * up_act).astype(jnp.bfloat16)
        partial_out = jnp.einsum(
            "secf,efd->secd", serve_inner_act, down_local, preferred_element_type=jnp.float32
        )
        result = split_pair(partial_out).astype(jnp.bfloat16)
        came_back, arrived, gate_act, up_act = (
            lax.all_to_all(result, "expert", split_axis=0, concat_axis=0, tiled=True),
            arrived_rows,
            gate_act,
            up_act,
        )
        picked = (
            came_back.reshape(experts * capacity, -1)[slot_index]
            .reshape(group_rows, TOP, -1)
            .astype(jnp.float32)
        )
        expert_sum = jnp.sum(picked * gate_weights[layer_index][:, :, None], axis=1)
        expert_sum = join_pair(expert_sum)
        stream = hidden + expert_sum
        kept_state.append(
            (
                stream_in,
                inverse_attn,
                gain_attention,
                normed,
                query_group,
                key_rot,
                value_heads,
                log_total,
                mixed_heads,
                query_full,
                key_full,
                value_full,
                out_full,
                hidden,
                inverse_exp,
                gain_expert,
                slot_index,
                slot_owner,
                slot_gate,
                arrived,
                gate_act,
                up_act,
            )
        )
    block_out = lax.dynamic_slice_in_dim(stream, blk_place * half_width, half_width, 1).astype(
        jnp.bfloat16
    )
    upstream = gather_directly(cotangent, "blk", 1).astype(jnp.float32)
    attention_parts = []
    expert_parts = []
    for layer_index in reversed(range(LAYERS)):
        (
            stream_in,
            inverse_attn,
            gain_attention,
            normed,
            query_group,
            key_rot,
            value_heads,
            log_total,
            mixed_heads,
            query_full,
            key_full,
            value_full,
            out_full,
            hidden,
            inverse_exp,
            gain_expert,
            slot_index,
            slot_owner,
            slot_gate,
            arrived,
            gate_act,
            up_act,
        ) = kept_state[layer_index]
        gate_local = gate_weight[layer_index]
        up_local = up_weight[layer_index]
        down_local = down_weight[layer_index]
        slot_grad = (
            (slot_gate[:, None] * upstream[slot_owner])
            .astype(jnp.bfloat16)
            .reshape(expert_count, -1, capacity, full_width)
        )
        slot_grad = lax.dynamic_slice_in_dim(slot_grad, blk_place * half_width, half_width, 3)
        incoming = lax.all_to_all(slot_grad, "expert", split_axis=0, concat_axis=0, tiled=True)
        incoming = widen_rows(incoming)
        sigmoid_gate = jax.nn.sigmoid(gate_act)
        inner_act = (gate_act * sigmoid_gate * up_act).astype(jnp.bfloat16)
        grad_down = jnp.einsum(
            "secf,secd->efd", inner_act, incoming, preferred_element_type=jnp.float32
        )
        inner_grad = jnp.einsum(
            "secd,efd->secf", incoming, down_local, preferred_element_type=jnp.float32
        )
        gate_grad = (
            inner_grad * up_act * sigmoid_gate * (1.0 + gate_act * (1.0 - sigmoid_gate))
        ).astype(jnp.bfloat16)
        up_grad = (inner_grad * gate_act * sigmoid_gate).astype(jnp.bfloat16)
        grad_gate = jnp.einsum(
            "secd,secf->edf", arrived, gate_grad, preferred_element_type=jnp.float32
        )
        grad_up = jnp.einsum("secd,secf->edf", arrived, up_grad, preferred_element_type=jnp.float32)
        row_partial = jnp.einsum(
            "secf,edf->secd", gate_grad, gate_local, preferred_element_type=jnp.float32
        )
        row_partial = row_partial + jnp.einsum(
            "secf,edf->secd", up_grad, up_local, preferred_element_type=jnp.float32
        )
        row_grad = split_pair(row_partial).astype(jnp.bfloat16)
        back_rows = lax.all_to_all(row_grad, "expert", split_axis=0, concat_axis=0, tiled=True)
        back_rows = back_rows.reshape(experts * capacity, -1)
        normed_grad = jnp.sum(
            back_rows[slot_index].reshape(group_rows, TOP, -1).astype(jnp.float32), axis=1
        )
        normed_grad = join_pair(normed_grad)
        through, grad_gain_exp = norm_back(
            hidden, inverse_exp, gain_expert.astype(jnp.float32), normed_grad
        )
        hidden_grad = upstream + through
        mixed_grad_in = hidden_grad.astype(jnp.bfloat16)
        grad_out = jnp.einsum(
            "tq,td->qd", mixed_heads, mixed_grad_in, preferred_element_type=jnp.float32
        )
        kv_local = key_rot.shape[1]
        head_share = query_group.shape[2]
        local_heads = kv_local * head_share
        mixed_grad = (
            jnp.einsum("td,qd->tq", mixed_grad_in, out_full, preferred_element_type=jnp.float32)
            .astype(jnp.bfloat16)
            .reshape(group_rows, kv_local, head_share, HEAD)
        )
        raw_scores = (
            jnp.einsum("qhgd,khd->hgqk", query_group, key_rot, preferred_element_type=jnp.float32)
            * score_scale
        )
        masked = jnp.where(allowed, raw_scores, -1e30)
        prob_full = jnp.exp(masked - log_total)
        prob_grad = jnp.einsum(
            "qhgd,khd->hgqk", mixed_grad, value_heads, preferred_element_type=jnp.float32
        )
        centre = jnp.sum(prob_full * prob_grad, axis=-1, keepdims=True)
        score_grad = (prob_full * (prob_grad - centre)).astype(jnp.bfloat16)
        query_grad = (
            jnp.einsum("hgqk,khd->qhgd", score_grad, key_rot, preferred_element_type=jnp.float32)
            * score_scale
        )
        key_grad = (
            jnp.einsum(
                "hgqk,qhgd->khd", score_grad, query_group, preferred_element_type=jnp.float32
            )
            * score_scale
        )
        value_grad = jnp.einsum(
            "hgqk,qhgd->khd",
            prob_full.astype(jnp.bfloat16),
            mixed_grad,
            preferred_element_type=jnp.float32,
        )
        query_lin = (
            unrotate(
                query_grad.reshape(group_rows, local_heads, HEAD),
                cosine_table[:, None],
                sine_table[:, None],
            )
            .reshape(group_rows, local_heads * HEAD)
            .astype(jnp.bfloat16)
        )
        key_lin = (
            unrotate(key_grad, cosine_table[:, None], sine_table[:, None])
            .reshape(group_rows, kv_local * HEAD)
            .astype(jnp.bfloat16)
        )
        value_lin = value_grad.reshape(group_rows, kv_local * HEAD).astype(jnp.bfloat16)
        grad_query = jnp.einsum("td,tq->dq", normed, query_lin, preferred_element_type=jnp.float32)
        grad_key = jnp.einsum("td,tq->dq", normed, key_lin, preferred_element_type=jnp.float32)
        grad_value = jnp.einsum("td,tq->dq", normed, value_lin, preferred_element_type=jnp.float32)
        normed_back = jnp.einsum(
            "tq,dq->td", query_lin, query_full, preferred_element_type=jnp.float32
        )
        normed_back = normed_back + jnp.einsum(
            "tq,dq->td", key_lin, key_full, preferred_element_type=jnp.float32
        )
        normed_back = pair_grad(
            normed_back
            + jnp.einsum("tq,dq->td", value_lin, value_full, preferred_element_type=jnp.float32)
        )
        through, grad_gain_attn = norm_back(
            stream_in, inverse_attn, gain_attention.astype(jnp.float32), normed_back
        )
        upstream = hidden_grad + through
        attention_parts.insert(
            0, (grad_gain_attn, grad_query, grad_key, grad_value, grad_out, grad_gain_exp)
        )
        expert_parts.insert(0, (grad_gate, grad_up, grad_down))
    stacked_gain_attn = jnp.stack([member[0] for member in attention_parts])
    stacked_query = jnp.stack([member[1] for member in attention_parts])
    stacked_key = jnp.stack([member[2] for member in attention_parts])
    stacked_value = jnp.stack([member[3] for member in attention_parts])
    stacked_out = jnp.stack([member[4] for member in attention_parts])
    stacked_gain_exp = jnp.stack([member[5] for member in attention_parts])
    stacked_gate = jnp.stack([member[0] for member in expert_parts])
    stacked_up = jnp.stack([member[1] for member in expert_parts])
    stacked_down = jnp.stack([member[2] for member in expert_parts])
    stacked_gain_attn, stacked_query, stacked_key, stacked_value, stacked_out, stacked_gain_exp = (
        *sent_together(
            (stacked_gain_attn, stacked_query, stacked_key, stacked_value), ("dp", "expert"), 1, 2
        ),
        lax.psum_scatter(stacked_out, ("dp", "expert"), scatter_dimension=2, tiled=True),
        lax.psum_scatter(stacked_gain_exp, ("dp", "expert"), scatter_dimension=1, tiled=True),
    )
    stacked_gate, stacked_up, stacked_down = (
        *tuple(
            (
                part.astype(jnp.float32)
                for part in in_one_piece(
                    (stacked_gate.astype(jnp.bfloat16), stacked_up.astype(jnp.bfloat16)), "dp", 2, 0
                )
            )
        ),
        lax.psum_scatter(
            stacked_down.astype(jnp.bfloat16), "dp", scatter_dimension=3, tiled=True
        ).astype(jnp.float32),
    )
    grad_tokens = lax.dynamic_slice_in_dim(upstream, blk_place * half_width, half_width, 1)
    return (
        block_out,
        grad_tokens,
        stacked_gain_attn,
        stacked_query,
        stacked_key,
        stacked_value,
        stacked_out,
        stacked_gain_exp,
        stacked_gate,
        stacked_up,
        stacked_down,
    )


def solution(mesh):
    placed = (
        P(("dp", "expert"), "blk"),
        P(("dp", "expert"), None),
        P(None, ("dp", "expert"), None),
        P(None, ("dp", "expert"), None),
        P(None, ("dp", "expert")),
        P(None, ("dp", "expert"), "blk"),
        P(None, ("dp", "expert"), "blk"),
        P(None, ("dp", "expert"), "blk"),
        P(None, "blk", ("dp", "expert")),
        P(None, ("dp", "expert")),
        P(None, "expert", None, "blk"),
        P(None, "expert", None, "blk"),
        P(None, "expert", "blk", None),
        P(("dp", "expert"), "blk"),
    )
    return jax.shard_map(
        per_device,
        mesh=mesh,
        in_specs=placed,
        out_specs=(
            P(("dp", "expert"), "blk"),
            P(("dp", "expert"), "blk"),
            P(None, ("dp", "expert")),
            P(None, ("dp", "expert"), "blk"),
            P(None, ("dp", "expert"), "blk"),
            P(None, ("dp", "expert"), "blk"),
            P(None, "blk", ("dp", "expert")),
            P(None, ("dp", "expert")),
            P(None, "expert", "dp", "blk"),
            P(None, "expert", "dp", "blk"),
            P(None, "expert", "blk", "dp"),
        ),
        check_vma=False,
    )
```

profile of v0, /device:TPU:0, one launch (start us, length us, event | category | flops | bytes accessed | tf_op | source)
XLA Modules:
  0.0 1110.5 jit_solution(6571557205723759953)
XLA Ops:
  13.0 4.0 all_to_all.110
  19.1 66.9 %all-gather.11.cloned.1.call-done = bf16[1536,1794]{1,0:T(8,128)(2,1)} async-done(((bf16[24,1794]{1,0:T(8,128)(2,1)}), bf16[1536,1794]{1,0:T(8,128)(2,1)}) %all-gather.11.cloned.1.call-update) | async-done | bytes 5511184 | tf_op jit(solution)/shard_map/all_gather | solution.py:50
  89.4 3.2 slice_bitcast_fusion.1
  92.6 4.3 copy.346
  101.8 3.5 fusion.36
  120.7 3.8 gather_fusion
  126.2 26.4 %all_to_all.111 = bf16[16,2,24,768]{3,2,1,0:T(8,128)(2,1)S(1)} all-to-all(bf16[16,2,24,768]{3,2,1,0:T(8,128)(2,1)S(1)} %dynamic-slice_select_fusion.1), channel_id=1, replica_groups=mesh['dp'=4,'expert'=16,'blk'=2] {'expert'}, dimensions={0} | all-to-all | bytes 2359296 | tf_op jit(solution)/shard_map/all_to_all | solution.py:254
  152.8 6.0 all_to_all.112
  165.2 6.5 all_to_all.113
  175.3 3.7 all-to-all-start.4
  180.3 3.2 scatter_custom_fusion.3
  183.5 27.9 %all-gather.13.cloned.1.call-done = bf16[1536,1794]{1,0:T(8,128)(2,1)} async-done(((bf16[24,1794]{1,0:T(8,128)(2,1)}), bf16[1536,1794]{1,0:T(8,128)(2,1)}) %all-gather.13.cloned.1.call-update) | async-done | bytes 5511184 | tf_op jit(solution)/shard_map/all_gather | solution.py:50
  214.2 3.2 slice_bitcast_fusion
  217.4 4.3 copy.367
  221.7 2.7 gather_fusion.1
  228.1 4.4 all_to_all.114
  233.2 4.2 all-to-all-start.11
  247.9 3.5 fusion.30
  260.4 4.3 gather_fusion.4
  264.7 2.9 fusion.7
  267.6 4.7 all-to-all-start.12
  275.0 17.4 %all-to-all-done.12 = bf16[16,2,24,768]{3,2,1,0:T(8,128)(2,1)} async-done(((bf16[16,2,24,768]{3,2,1,0:T(8,128)(2,1)}), bf16[16,2,24,768]{3,2,1,0:T(8,128)(2,1)}, u32[]{:S(2)}, u32[]{:S(2)}) %all-to-all-start.12) | async-done | bytes 1179680 | tf_op jit(solution)/shard_map/all_to_all | solution.py:347
  295.3 4.9 all-to-all-start.13
  308.9 3.8 gather_fusion.2
  312.7 2.6 dynamic-slice_select_fusion
  315.3 4.4 all-to-all-start.6
  319.7 3.3 copy.485
  323.0 17.4 %all-to-all-done.6 = bf16[16,2,24,768]{3,2,1,0:T(8,128)(2,1)} async-done(((bf16[16,2,24,768]{3,2,1,0:T(8,128)(2,1)}), bf16[16,2,24,768]{3,2,1,0:T(8,128)(2,1)}, u32[]{:S(2)}, u32[]{:S(2)}) %all-to-all-start.6) | async-done | bytes 1179680 | tf_op jit(solution)/shard_map/all_to_all | solution.py:254
  341.9 6.4 all_to_all.115
  358.2 6.5 all_to_all.116
  368.2 3.7 all-to-all-start.15
  374.6 17.2 %all-to-all-done.15 = bf16[16,2,24,768]{3,2,1,0:T(8,128)(2,1)S(1)} async-done(((bf16[16,2,24,768]{3,2,1,0:T(8,128)(2,1)}), bf16[16,2,24,768]{3,2,1,0:T(8,128)(2,1)S(1)}, u32[]{:S(2)}, u32[]{:S(2)}) %all-to-all-start.15) | async-done | bytes 1179680 | tf_op jit(solution)/shard_map/all_to_all | solution.py:372
  391.8 2.8 gather_fusion.5
  394.7 2.6 reshape.899
  399.7 5.4 all_to_all.117
  426.3 7.0 all-gather.19.cloned.1.call-done
  442.0 4.2 gather_fusion.6
  448.2 25.7 %all_to_all.118 = bf16[16,2,24,768]{3,2,1,0:T(8,128)(2,1)S(1)} all-to-all(bf16[16,2,24,768]{3,2,1,0:T(8,128)(2,1)S(1)} %fusion.6), channel_id=1, replica_groups=mesh['dp'=4,'expert'=16,'blk'=2] {'expert'}, dimensions={0} | all-to-all | bytes 2359296 | tf_op jit(solution)/shard_map/all_to_all | solution.py:347
  474.2 6.2 all_to_all.119
  485.6 6.5 all_to_all.120
  495.5 3.9 all-to-all-start.20
  499.5 19.8 %all-to-all-done.20 = bf16[16,2,24,768]{3,2,1,0:T(8,128)(2,1)S(1)} async-done(((bf16[16,2,24,768]{3,2,1,0:T(8,128)(2,1)}), bf16[16,2,24,768]{3,2,1,0:T(8,128)(2,1)S(1)}, u32[]{:S(2)}, u32[]{:S(2)}) %all-to-all-start.20) | async-done | bytes 1179680 | tf_op jit(solution)/shard_map/all_to_all | solution.py:372
  519.3 2.9 gather_fusion.7
  527.2 5.1 all_to_all.121
  547.1 3.2 fusion.5
  551.8 2.6 pad_maximum_fusion.3
  554.4 12.6 %copy.469 = bf16[2,2,384,1536]{2,1,0,3:T(2,128)(2,1)} copy(bf16[2,2,384,1536]{3,2,1,0:T(8,128)(2,1)} %pad_maximum_fusion.3) | data formatting | bytes 9437184
  567.0 11.2 %reshape.1051 = bf16[1536,1536]{1,0:T(8,128)(2,1)} reshape(bf16[1536,2,2,384]{3,2,1,0:T(2,128)(2,1)} %bitcast.641) | data formatting | bytes 9437184
  579.3 3.5 fusion.3
  587.9 4.9 pad_maximum_fusion.2
  595.3 2.9 convolution_bitcast_fusion.2
  602.4 4.6 pad_maximum_fusion.1
  606.9 14.9 %copy.419 = f32[2,768,1536]{1,0,2:T(2,128)} copy(f32[2,768,1536]{2,1,0:T(8,128)} %pad_maximum_fusion.1) | data formatting | bytes 18874368 | tf_op jit(solution)/shard_map/stack | solution.py:461
  625.6 4.6 pad_maximum_fusion
  633.7 35.7 %concatenate.75 = f32[2,1536,1025]{1,2,0:T(8,128)} concatenate(f32[2,1536,1]{1,2,0:T(1,128)S(1)} %reshape.887, f32[2,1536,768]{1,2,0:T(8,128)} %pad_maximum_fusion, f32[2,1536,128]{1,2,0:T(8,128)} %pad_maximum_fusion.4, f32[2,1536,128]{1,2,0:T(8,128)S(1)} %pad_maximum_fusion.5), dimensions={2} | concatenate | bytes 25190400 | tf_op jit(solution)/shard_map/concatenate | solution.py:60
  669.4 21.3 %copy.417 = f32[2,1536,1025]{2,0,1:T(2,128)} copy(f32[2,1536,1025]{1,2,0:T(8,128)} %concatenate.75) | data formatting | bytes 25190400 | tf_op jit(solution)/shard_map/concatenate | solution.py:60
  691.7 3.1 convolution_convert_fusion
  695.0 5.6 all_to_all.122
  702.9 3.9 all-to-all-start.9
  708.9 17.7 %all-to-all-done.9 = bf16[16,2,24,768]{3,2,1,0:T(8,128)(2,1)S(1)} async-done(((bf16[16,2,24,768]{3,2,1,0:T(8,128)(2,1)}), bf16[16,2,24,768]{3,2,1,0:T(8,128)(2,1)S(1)}, u32[]{:S(2)}, u32[]{:S(2)}) %all-to-all-start.9) | async-done | bytes 1179680 | tf_op jit(solution)/shard_map/all_to_all | solution.py:268
  730.7 4.6 all_to_all.123
  736.2 348.4 %all-reduce.2 = f32[2,1536]{1,0:T(2,128)S(1)} all-reduce(f32[2,1536]{1,0:T(2,128)S(1)} %pad_maximum_fusion.11), channel_id=8, replica_groups=mesh['dp'=4,'expert'=16,'blk'=2] {'dp','expert'}, use_global_device_ids=true, to_apply=%region_47.48.clone | all-reduce | flops 3072 | bytes 24576
  1086.2 2.9 reshape.1052
  1092.6 4.1 slice_convert_fusion
  (663 shorter events, 207.1 us)
Async XLA Ops:
  7.2 78.8 %all-gather.11.cloned.1.call-start = ((), (), s32[]{:S(2)}) async-start(), calls=%async_computation.24 | async-start | bytes 5990400 | tf_op jit(solution)/shard_map/all_gather | solution.py:50
  12.0 105.0 %all-gather.15.cloned.1.call-start = ((), (), s32[]{:S(2)}) async-start(), calls=%async_computation.27 | async-start | bytes 2359296 | tf_op jit(solution)/shard_map/all_gather | solution.py:16
  17.6 102.0 %copy-start.6 = (f32[128,1536]{1,0:T(8,128)}, f32[128,1536]{1,0:T(8,128)S(1)}, u32[]{:S(2)}) copy-start(f32[128,1536]{1,0:T(8,128)S(1)} %copy.454) | copy-start | bytes 2359300
  18.7 81.2 %copy-start.123 = (f32[128]{0:T(128)}, f32[128]{0:T(128)S(1)}, u32[]{:S(2)}) copy-start(f32[128]{0:T(128)S(1)} %get-tuple-element.150) | copy-start | bytes 1540
  18.8 80.7 %copy-start.95 = (pred[128,128]{0,1:T(8,128)(4,1)}, pred[128,128]{0,1:T(8,128)(4,1)S(1)}, u32[]{:S(2)}) copy-start(pred[128,128]{0,1:T(8,128)(4,1)S(1)} %compare_and_fusion) | copy-start | bytes 49156
  19.1 80.3 %copy-start.57 = (f32[128,64]{0,1:T(8,128)}, f32[128,64]{0,1:T(8,128)S(1)}, u32[]{:S(2)}) copy-start(f32[128,64]{0,1:T(8,128)S(1)} %get-tuple-element.148) | copy-start | bytes 98308
  19.1 80.3 %copy-start.61 = (f32[128,64]{0,1:T(8,128)}, f32[128,64]{0,1:T(8,128)S(1)}, u32[]{:S(2)}) copy-start(f32[128,64]{0,1:T(8,128)S(1)} %get-tuple-element.147) | copy-start | bytes 98308
  87.6 12.3 %copy-start.93 = (f32[1536]{0:T(1024)}, f32[1536]{0:T(1024)S(1)}, u32[]{:S(2)}) copy-start(f32[1536]{0:T(1024)S(1)} %get-tuple-element.80) | copy-start | bytes 18436
  87.9 9.0 copy-start.10
  105.4 106.0 %all-gather.13.cloned.1.call-start = ((), (), s32[]{:S(2)}) async-start(), calls=%async_computation.25 | async-start | bytes 5990400 | tf_op jit(solution)/shard_map/all_gather | solution.py:50
  110.4 6.5 copy-start.150
  124.5 34.6 %slice-start.8 = ((s8[4718592]{0:T(1024)(128)(4,1)}), s8[4194304]{0:T(1024)(128)(4,1)S(1)}, s32[]{:S(2)}) async-start(s8[4718592]{0:T(1024)(128)(4,1)} %bitcast.679), calls=%async_computation.41 | async-start | bytes 8388608
  152.6 6.5 slice-start.9
  152.8 7.8 slice-start.2
  174.1 9.3 copy-start.133
  175.3 46.4 %all-to-all-start.4 = ((bf16[16,2,24,768]{3,2,1,0:T(8,128)(2,1)}), bf16[16,2,24,768]{3,2,1,0:T(8,128)(2,1)S(1)}, u32[]{:S(2)}, u32[]{:S(2)}) async-start(bf16[16,2,24,768]{3,2,1,0:T(8,128)(2,1)} %copy.361), calls=%async_computation.4 | async-start | bytes 2359296 | tf_op jit(solution)/shard_map/all_to_all | solution.py:268
  183.5 38.2 %copy-start.122 = (s32[1024]{0:T(1024)}, s32[1024]{0:T(1024)S(1)}, u32[]{:S(2)}) copy-start(s32[1024]{0:T(1024)S(1)} %pad_clamp_fusion.2) | copy-start | bytes 12292
  226.1 6.4 copy-start.92
  233.2 22.3 %all-to-all-start.11 = ((bf16[2,128,768]{2,1,0:T(8,128)(2,1)}), bf16[2,128,768]{2,1,0:T(8,128)(2,1)}, u32[]{:S(2)}, u32[]{:S(2)}) async-start(bf16[2,128,768]{2,1,0:T(8,128)(2,1)} %broadcast_in_dim.95), calls=%async_computation.11 | async-start | bytes 786432 | tf_op jit(solution)/shard_map/all_to_all | solution.py:28
  237.4 62.8 %all-gather.17.cloned.1.call-start = ((), (), s32[]{:S(2)}) async-start(), calls=%async_computation.28 | async-start | bytes 2359296 | tf_op jit(solution)/shard_map/all_gather | solution.py:16
  241.3 63.8 %copy-start = (f32[128,2,768]{0,2,1:T(8,128)}, f32[128,2,768]{0,2,1:T(8,128)S(1)}, u32[]{:S(2)}) copy-start(f32[128,2,768]{0,2,1:T(8,128)S(1)} %get-tuple-element.96) | copy-start | bytes 2359300
  245.4 5.9 copy-start.8
  256.7 8.0 copy-start.23
  267.6 24.8 %all-to-all-start.12 = ((bf16[16,2,24,768]{3,2,1,0:T(8,128)(2,1)}), bf16[16,2,24,768]{3,2,1,0:T(8,128)(2,1)}, u32[]{:S(2)}, u32[]{:S(2)}) async-start(bf16[16,2,24,768]{3,2,1,0:T(8,128)(2,1)} %fusion.7), calls=%async_computation.12 | async-start | bytes 2359296 | tf_op jit(solution)/shard_map/all_to_all | solution.py:347
  295.3 20.0 %all-to-all-start.13 = ((bf16[2,16,2,24,768]{4,3,1,2,0:T(8,128)(2,1)}), bf16[2,16,2,24,768]{4,3,1,2,0:T(8,128)(2,1)}, u32[]{:S(2)}, u32[]{:S(2)}) async-start(bf16[2,16,2,24,768]{4,3,1,2,0:T(8,128)(2,1)} %broadcast_in_dim.96), calls=%async_computation.13 | async-start | bytes 4718592 | tf_op jit(solution)/shard_map/all_to_all | solution.py:28
  315.3 25.0 %all-to-all-start.6 = ((bf16[16,2,24,768]{3,2,1,0:T(8,128)(2,1)}), bf16[16,2,24,768]{3,2,1,0:T(8,128)(2,1)}, u32[]{:S(2)}, u32[]{:S(2)}) async-start(bf16[16,2,24,768]{3,2,1,0:T(8,128)(2,1)} %dynamic-slice_select_fusion), calls=%async_computation.6 | async-start | bytes 2359296 | tf_op jit(solution)/shard_map/all_to_all | solution.py:254
  341.7 6.8 slice-start.4
  341.9 6.7 slice-start.5
  341.9 8.1 slice-start.10
  368.2 23.6 %all-to-all-start.15 = ((bf16[16,2,24,768]{3,2,1,0:T(8,128)(2,1)}), bf16[16,2,24,768]{3,2,1,0:T(8,128)(2,1)S(1)}, u32[]{:S(2)}, u32[]{:S(2)}) async-start(bf16[16,2,24,768]{3,2,1,0:T(8,128)(2,1)} %copy.392), calls=%async_computation.15 | async-start | bytes 2359296 | tf_op jit(solution)/shard_map/all_to_all | solution.py:372
  372.0 61.3 %all-gather.19.cloned.1.call-start = ((), (), s32[]{:S(2)}) async-start(), calls=%async_computation.29 | async-start | bytes 2359296 | tf_op jit(solution)/shard_map/all_gather | solution.py:16
  399.6 7.8 copy-start.14
  399.7 7.8 copy-start.106
  399.7 7.8 copy-start.126
  422.7 15.4 %copy-start.1 = (f32[128,2,768]{0,2,1:T(8,128)S(1)}, f32[128,2,768]{0,2,1:T(8,128)}, u32[]{:S(2)}) copy-start(f32[128,2,768]{0,2,1:T(8,128)} %copy-done) | copy-start | bytes 2359300
  422.7 15.4 %copy-start.104 = (f32[2,768]{1,0:T(2,128)S(1)}, f32[2,768]{1,0:T(2,128)}, u32[]{:S(2)}) copy-start(f32[2,768]{1,0:T(2,128)} %reshape.895) | copy-start | bytes 18436
  422.7 15.4 %copy-start.118 = (f32[128]{0:T(128)S(1)}, f32[128]{0:T(128)}, u32[]{:S(2)}) copy-start(f32[128]{0:T(128)} %copy-done.117) | copy-start | bytes 1540
  433.3 7.1 copy-start.5
  433.3 7.1 copy-start.144
  446.2 34.4 %slice-start.18 = ((s8[4718592]{0:T(1024)(128)(4,1)}), s8[4194304]{0:T(1024)(128)(4,1)S(1)}, s32[]{:S(2)}) async-start(s8[4718592]{0:T(1024)(128)(4,1)} %bitcast.749), calls=%async_computation.51 | async-start | bytes 8388608
  474.0 6.6 slice-start.19
  474.0 6.6 copy-start.161
  474.1 6.6 copy-start.162
  474.2 8.2 slice-start.12
  474.2 9.7 slice-start.6
  495.5 23.8 %all-to-all-start.20 = ((bf16[16,2,24,768]{3,2,1,0:T(8,128)(2,1)}), bf16[16,2,24,768]{3,2,1,0:T(8,128)(2,1)S(1)}, u32[]{:S(2)}, u32[]{:S(2)}) async-start(bf16[16,2,24,768]{3,2,1,0:T(8,128)(2,1)} %copy.406), calls=%async_computation.20 | async-start | bytes 2359296 | tf_op jit(solution)/shard_map/all_to_all | solution.py:372
  499.5 130.7 %all-gather.21.cloned.1.call-start = ((), (), s32[]{:S(2)}) async-start(), calls=%async_computation.30 | async-start | bytes 2359296 | tf_op jit(solution)/shard_map/all_gather | solution.py:16
  527.2 6.6 copy-start.129
  547.0 539.1 %reduce-scatter.8.cloned.1.call-start = ((), (), s32[]{:S(2)}) async-start(), calls=%async_computation.31 | async-start | bytes 5898240
  578.3 514.3 %reduce-scatter.6.cloned.1.call-start = ((), (), s32[]{:S(2)}) async-start(), calls=%async_computation.26 | async-start | bytes 11796480 | tf_op jit(solution)/shard_map/reduce_scatter | solution.py:71
  592.9 503.9 %all-reduce.6.cloned.1.call-start = ((), (), s32[]{:S(2)}) async-start(), calls=%async_computation.32 | async-start | bytes 47185920
  606.9 14.9 %copy-start.11 = (bf16[128,2,768]{0,2,1:T(8,128)(2,1)S(1)}, bf16[128,2,768]{0,2,1:T(8,128)(2,1)}, u32[]{:S(2)}) copy-start(bf16[128,2,768]{0,2,1:T(8,128)(2,1)} %copy-done.10) | copy-start | bytes 1179652
  606.9 14.9 %copy-start.78 = (bf16[128,128]{0,1:T(8,128)(2,1)S(1)}, bf16[128,128]{0,1:T(8,128)(2,1)}, u32[]{:S(2)}) copy-start(bf16[128,128]{0,1:T(8,128)(2,1)} %copy-done.77) | copy-start | bytes 98308
  606.9 15.2 %copy-start.82 = (bf16[128,128]{0,1:T(8,128)(2,1)S(1)}, bf16[128,128]{0,1:T(8,128)(2,1)}, u32[]{:S(2)}) copy-start(bf16[128,128]{0,1:T(8,128)(2,1)} %copy-done.81) | copy-start | bytes 98308
  631.8 37.6 %copy-start.25 = (f32[128,1536]{1,0:T(8,128)}, f32[128,1536]{1,0:T(8,128)S(1)}, u32[]{:S(2)}) copy-start(f32[128,1536]{1,0:T(8,128)S(1)} %reduce_sum.337) | copy-start | bytes 2359300
  701.8 7.0 copy-start.94
  701.8 24.9 %copy-start.121 = (s32[1024]{0:T(1024)S(1)}, s32[1024]{0:T(1024)}, u32[]{:S(2)}) copy-start(s32[1024]{0:T(1024)} %pad_clamp_fusion) | copy-start | bytes 12292
  702.9 23.8 %all-to-all-start.9 = ((bf16[16,2,24,768]{3,2,1,0:T(8,128)(2,1)}), bf16[16,2,24,768]{3,2,1,0:T(8,128)(2,1)S(1)}, u32[]{:S(2)}, u32[]{:S(2)}) async-start(bf16[16,2,24,768]{3,2,1,0:T(8,128)(2,1)} %copy.382), calls=%async_computation.9 | async-start | bytes 2359296 | tf_op jit(solution)/shard_map/all_to_all | solution.py:268
  730.6 354.6 %copy-start.152 = (f32[128]{0:T(128)S(1)}, f32[128]{0:T(128)}, u32[]{:S(2)}) copy-start(f32[128]{0:T(128)} %get-tuple-element.88) | copy-start | bytes 1540
  730.7 354.6 %copy-start.7 = (f32[128,1536]{1,0:T(8,128)S(1)}, f32[128,1536]{1,0:T(8,128)}, u32[]{:S(2)}) copy-start(f32[128,1536]{1,0:T(8,128)} %copy-done.6) | copy-start | bytes 2359300
  730.7 354.6 %copy-start.26 = (f32[128,1536]{1,0:T(8,128)S(1)}, f32[128,1536]{1,0:T(8,128)}, u32[]{:S(2)}) copy-start(f32[128,1536]{1,0:T(8,128)} %copy-done.25) | copy-start | bytes 2359300
  730.7 354.5 %copy-start.44 = (f32[128,1536]{1,0:T(8,128)S(1)}, f32[128,1536]{1,0:T(8,128)}, u32[]{:S(2)}) copy-start(f32[128,1536]{1,0:T(8,128)} %copy-done.43) | copy-start | bytes 2359300
  730.7 354.5 %copy-start.124 = (f32[128]{0:T(128)S(1)}, f32[128]{0:T(128)}, u32[]{:S(2)}) copy-start(f32[128]{0:T(128)} %copy-done.123) | copy-start | bytes 1540
  730.7 354.5 %copy-start.151 = (f32[128]{0:T(128)S(1)}, f32[128]{0:T(128)}, u32[]{:S(2)}) copy-start(f32[128]{0:T(128)} %get-tuple-element.149) | copy-start | bytes 1540
  (136 other events, 358.3 us)
Sparse Core Ops, SparseCore 0:
  12.1 73.8 all-gather.10
  105.5 11.3 all-gather.14
  120.3 91.0 all-gather.12
  251.5 11.5 all-gather.16
  422.9 10.3 all-gather.18
  547.1 10.3 all-gather.20
  578.4 48.8 reduce-scatter.7
  629.8 88.6 reduce-scatter.5
  724.3 258.9 all-reduce.5
where the time goes:
time: 1130 us; the launch traced here: 1110 us
  blocking collectives  468 us (41%)
  local copies, waits for them, and re-layouts  230 us (20%)
  waiting for transfers between devices  191 us (17%)
  other arithmetic  92.5 us (8%)
  matrix products  76.7 us (7%)
  starting transfers between devices  34.6 us (3%)
  between operations  17.8 us (2%)
    unnamed x1, blocking collectives  348 us
    all_gather x2, waiting for transfers between devices, gather_turned(): lax.all_gather(both, axis, axis=0, tiled=True)  94.8 us
    concatenate x2, local copies, waits for them, and re-layouts, sent_together(): both = jnp.concatenate(columns, axis=along)  56.9 us
    unnamed x381, local copies, waits for them, and re-layouts  44.3 us
    all_to_all x8, blocking collectives, copy_for_each(): return lax.all_to_all(copies, axis, split_axis=0, concat_axis=0, tiled=True)  42.2 us
    all_to_all x2, waiting for transfers between devices, per_device(): lax.all_to_all(row_grad, 'expert', split_axis=0, concat_axis=0, tiled=True)  37 us
    all_to_all x1, blocking collectives, per_device(): lax.all_to_all(outgoing, 'expert', split_axis=0, concat_axis=0, tiled=True)  26.4 us
    all_to_all x1, blocking collectives, per_device(): lax.all_to_all(slot_grad, 'expert', split_axis=0, concat_axis=0, tiled=True)  25.7 us
  transfers between devices with their start and end apart: 17, of which 8 were waited for; matrix products, arithmetic and copies ran while one was open for 24% of the time, Pallas kernels for 0%

commit v1 on v0

v1 whole, which is shorter than its diff:
```python
import functools

import jax
import jax.numpy as jnp
from jax import lax
from jax.experimental import pallas as pl
from jax.experimental.pallas import tpu as pltpu
from jax.sharding import PartitionSpec as P

HEAD = 128
TOP = 4
LAYERS = 2
F32 = jnp.float32
BF = jnp.bfloat16
MESH = pl.DeviceIdType.MESH

epsilon = 1e-06
rope_base = 1000000.0

TOKENS = 128
WIDE = 1536
HALF = WIDE // 2
HEADS = 6
HIDDEN = 384
PEERS = 16
CAP = 24
SLOTS = PEERS * CAP
SHARD = 24
QKV = 1024
OUT = 768
COLS = QKV + OUT + 128
PART = COLS // 3
ORDERS = ((0, 1, 2), (1, 2, 0), (2, 0, 1))
LIMIT = 60 << 20

ANY = pl.BlockSpec(memory_space=pl.ANY)
VMEM = pl.BlockSpec(memory_space=pltpu.VMEM)


def dot(a, b, ca=1, cb=0):
    return lax.dot_general(a, b, (((ca,), (cb,)), ((), ())), preferred_element_type=F32)


def coords():
    ex = lax.axis_index("expert")
    return [lax.axis_index("dp"), lax.div(ex, 4), lax.rem(ex, 4)]


def shifted(xyz, axis, by):
    moved = list(xyz)
    moved[axis] = lax.rem(xyz[axis] + by, 4)
    return moved


def device_at(xyz, core):
    return (xyz[0], xyz[1] * 4 + xyz[2], core)


def partner():
    return (lax.axis_index("dp"), lax.axis_index("expert"), 1 - lax.axis_index("blk"))


def greet(devices):
    barrier = pltpu.get_barrier_semaphore()
    for device in devices:
        pl.semaphore_signal(barrier, inc=1, device_id=device, device_id_type=MESH)
    pl.semaphore_wait(barrier, len(devices))


def peer(step):
    dp, ex, core = (lax.axis_index(a) for a in ("dp", "expert", "blk"))
    return (dp, lax.rem(ex + step, PEERS), core)


def greet_peers():
    greet([peer(d) for d in range(1, PEERS)] + [partner()])


class Sender:
    def __init__(self, send, recv):
        self.send, self.recv, self.at = send, recv, 0

    def start(self, src, dst, device):
        assert self.at < self.send.shape[0]
        copy = pltpu.make_async_remote_copy(
            src_ref=src,
            dst_ref=dst,
            send_sem=self.send.at[self.at],
            recv_sem=self.recv.at[self.at],
            device_id=device,
            device_id_type=MESH,
        )
        self.at += 1
        copy.start()
        return copy


def exchange_copy(src, dst, send, recv, step):
    me = lax.axis_index("expert")
    target = peer(step)
    return pltpu.make_async_remote_copy(
        src_ref=src.at[target[1]],
        dst_ref=dst.at[me],
        send_sem=send.at[step],
        recv_sem=recv.at[step],
        device_id=target,
        device_id_type=MESH,
    )


def exchange_start(src, dst, send, recv):
    me = lax.axis_index("expert")

    def begin(step, carry):
        exchange_copy(src, dst, send, recv, step).start()
        return carry

    lax.fori_loop(1, PEERS, begin, 0)
    pltpu.make_async_copy(src.at[me], dst.at[me], send.at[0]).start()


def exchange_wait(src, dst, send, recv):
    me = lax.axis_index("expert")

    def end(step, carry):
        exchange_copy(src, dst, send, recv, step).wait()
        return carry

    lax.fori_loop(1, PEERS, end, 0)
    pltpu.make_async_copy(src.at[me], dst.at[me], send.at[0]).wait()


def rows_of(ref):
    return ref[...].astype(F32).reshape(SLOTS, WIDE).astype(BF)


def store_rows(ref, rows):
    ref[...] = rows.reshape(PEERS, CAP, WIDE).astype(BF)


def slot_matrices(ids, weights):
    core = lax.axis_index("blk")
    expert = 2 * lax.broadcasted_iota(jnp.int32, (PEERS, TOKENS), 0) + core
    chosen = jnp.zeros((PEERS, TOKENS), F32)
    gate = jnp.zeros((PEERS, TOKENS), F32)
    for j in range(TOP):
        hit = jnp.where(ids[j : j + 1, :] == expert, 1.0, 0.0)
        chosen = chosen + hit
        gate = gate + hit * weights[j : j + 1, :]
    before = lax.broadcasted_iota(jnp.int32, (TOKENS, TOKENS), 0) < lax.broadcasted_iota(
        jnp.int32, (TOKENS, TOKENS), 1
    )
    rank = dot(chosen.astype(BF), jnp.where(before, 1.0, 0.0).astype(BF))
    rank = jnp.where(chosen > 0.0, rank, -1.0)
    shape = (PEERS, CAP, TOKENS)
    place = lax.broadcasted_iota(jnp.int32, shape, 1).astype(F32)
    onehot = jnp.where(jnp.broadcast_to(rank[:, None, :], shape) == place, 1.0, 0.0)
    weighted = onehot * jnp.broadcast_to(gate[:, None, :], shape)
    return onehot.reshape(SLOTS, TOKENS), weighted.reshape(SLOTS, TOKENS)


def halves(value):
    high = value.astype(BF)
    return high, (value - high.astype(F32)).astype(BF)


def combine(weighted, rows):
    high, low = halves(weighted)
    return dot(high, rows, 0, 0) + dot(low, rows, 0, 0)


def gain_rows(w_ref):
    unit = jnp.where(
        lax.broadcasted_iota(jnp.int32, (8, 128), 0) == lax.broadcasted_iota(jnp.int32, (8, 128), 1),
        1.0,
        0.0,
    ).astype(BF)
    rows = dot(unit, w_ref[:, QKV + OUT : COLS], 1, 1)
    return rows[0:1, :], rows[1:2, :]


def inverse_norm(u):
    return lax.rsqrt(jnp.mean(u * u, axis=-1, keepdims=True) + epsilon)


def norm_back(u, inverse, gain, upstream):
    scaled = upstream * gain
    inward = inverse * scaled - u * (inverse * inverse * inverse) * jnp.mean(
        u * scaled, axis=-1, keepdims=True
    )
    return inward, upstream * u * inverse


def rotate(u, cos, sin):
    return u * cos + pltpu.roll(u, HEAD // 2, 1) * sin


def unrotate(u, cos, sin):
    return u * cos - pltpu.roll(u, HEAD // 2, 1) * sin


def head_of(value, h):
    return value[:, h * HEAD : (h + 1) * HEAD]


def attention(x, gain, w_ref, cos, sin, allow, n_ref, qkv_ref, prob_ref, o_ref):
    n = (x * inverse_norm(x) * gain).astype(BF)
    n_ref[...] = n
    flat = dot(n, w_ref[:, 0:QKV])
    for h in range(HEADS + 1):
        qkv_ref[:, h * HEAD : (h + 1) * HEAD] = rotate(head_of(flat, h), cos, sin).astype(BF)
    qkv_ref[:, (HEADS + 1) * HEAD :] = flat[:, (HEADS + 1) * HEAD :].astype(BF)
    key = qkv_ref[:, HEADS * HEAD : (HEADS + 1) * HEAD]
    value = qkv_ref[:, (HEADS + 1) * HEAD :]
    for h in range(HEADS):
        scores = dot(qkv_ref[:, h * HEAD : (h + 1) * HEAD], key, 1, 1) * HEAD ** (-0.5)
        scores = jnp.where(allow > 0.0, scores, -1e30)
        weight = jnp.exp(scores - jnp.max(scores, axis=-1, keepdims=True))
        prob = weight / jnp.sum(weight, axis=-1, keepdims=True)
        prob_ref[h] = prob
        o_ref[:, h * HEAD : (h + 1) * HEAD] = dot(prob.astype(BF), value).astype(BF)
    return dot(o_ref[...], w_ref[:, QKV : QKV + OUT], 1, 1)


def expert_weight_copies(layer, own, other, held, sem):
    core = lax.axis_index("blk")
    copies = []
    for i in range(3):
        copies.append(pltpu.make_async_copy(own[i].at[layer, core], held[i].at[0], sem.at[2 * i]))
        copies.append(pltpu.make_async_copy(other[i].at[layer], held[i].at[1], sem.at[2 * i + 1]))
    for copy in copies:
        copy.start()
    return copies


def expert_forward(rows, held, a_ref, b_ref):
    gate, up, down = held
    total = None
    for c in range(2):
        a = dot(rows, gate[c])
        b = dot(rows, up[c])
        a_ref[c] = a
        b_ref[c] = b
        z = (a / (1.0 + jnp.exp(-a)) * b).astype(BF)
        term = dot(z, down[c])
        total = term if total is None else total + term
    return total


def expert_backward(dy, held, a_ref, b_ref, z_ref, d_ref):
    gate, up, down = held
    total = None
    for c in range(2):
        a = a_ref[c]
        b = b_ref[c]
        sg = 1.0 / (1.0 + jnp.exp(-a))
        z_ref[:, c * HIDDEN : (c + 1) * HIDDEN] = (a * sg * b).astype(BF)
        dz = dot(dy, down[c], 1, 1)
        da = (dz * b * sg * (1.0 + a * (1.0 - sg))).astype(BF)
        db = (dz * a * sg).astype(BF)
        d_ref[:, 2 * c * HIDDEN : (2 * c + 1) * HIDDEN] = da
        d_ref[:, (2 * c + 1) * HIDDEN : (2 * c + 2) * HIDDEN] = db
        term = dot(da, gate[c], 1, 1) + dot(db, up[c], 1, 1)
        total = term if total is None else total + term
    return total


def expert_gradients(rows_ref, dy_ref, z_ref, d_ref, grad_ref):
    for q in range(4):
        columns = slice(q * HIDDEN, (q + 1) * HIDDEN)
        both = dot(rows_ref[:, columns], d_ref[...], 0, 0)
        for c in range(2):
            for i in range(2):
                at = (2 * c + i) * HIDDEN
                grad_ref[q, 3 * c + i] = both[:, at : at + HIDDEN].astype(BF)
        low = dot(z_ref[...], dy_ref[:, columns], 0, 0)
        for c in range(2):
            grad_ref[q, 3 * c + 2] = low[c * HIDDEN : (c + 1) * HIDDEN].astype(BF)


def gather_kernel(
    shard, tok, cot, gate, up, down, w0, w1, tok_all, cot_all, gate_o, up_o, down_o, send, recv, local
):
    xyz, core = coords(), lax.axis_index("blk")
    ring = [device_at(shifted(xyz, axis, by), core) for axis in range(3) for by in (1, 2, 3)]
    greet(ring + [partner()])
    sender = Sender(send, recv)
    whole = (w0, w1)
    mine = pl.ds(pl.multiple_of(core * HALF, HALF), HALF)
    here = [
        pltpu.make_async_copy(shard.at[l], whole[l].at[xyz[0], xyz[1], xyz[2]], local.at[l])
        for l in range(LAYERS)
    ]
    here.append(pltpu.make_async_copy(tok, tok_all.at[:, mine], local.at[2]))
    here.append(pltpu.make_async_copy(cot, cot_all.at[:, mine], local.at[3]))
    for copy in here:
        copy.start()
    others = []

    def slab(l, p, known, at, half=None):
        index = list(at)
        for axis in known:
            index[axis] = pl.ds(0, 4)
        if half is not None:
            index[known[0]] = pl.ds(2 * half, 2)
        return whole[l].at[index[0], index[1], index[2], :, pl.ds(p * PART, PART)]

    first = []
    for l in range(LAYERS):
        for p, order in enumerate(ORDERS):
            source = shard.at[l, :, pl.ds(p * PART, PART)]
            for by in (1, 3, 2):
                target = device_at(shifted(xyz, order[0], by), core)
                first.append(sender.start(source, slab(l, p, (), xyz), target))
    others.append(sender.start(tok, tok_all.at[:, mine], partner()))
    others.append(sender.start(cot, cot_all.at[:, mine], partner()))
    for ref, to in ((gate, gate_o), (up, up_o), (down, down_o)):
        for l in range(LAYERS):
            others.append(sender.start(ref.at[l, 1 - core], to.at[l], partner()))
    for copy in here + first:
        copy.wait()
    for stage in (1, 2):
        nears = []
        for l in range(LAYERS):
            for p, order in enumerate(ORDERS):
                known, axis = order[:stage], order[stage]
                block = slab(l, p, known, xyz)
                nears.append(
                    [
                        sender.start(block, block, device_at(shifted(xyz, axis, by), core))
                        for by in (1, 3)
                    ]
                )
        relays = []
        for l in range(LAYERS):
            for p, order in enumerate(ORDERS):
                known, axis = order[:stage], order[stage]
                for copy, by, half in zip(nears[l * 3 + p], (1, 3), (0, 1)):
                    copy.wait_recv()
                    block = slab(l, p, known, shifted(xyz, axis, 4 - by), half)
                    relays.append(
                        sender.start(block, block, device_at(shifted(xyz, axis, by), core))
                    )
        for pair in nears:
            for copy in pair:
                copy.wait_send()
        for copy in relays:
            copy.wait()
    for copy in others:
        copy.wait()


def attention_part(x, refs, part, theirs, pair):
    gain_a, gain_e = gain_rows(refs["w"])
    part[...] = attention(
        x,
        gain_a,
        refs["w"],
        refs["cos"][...],
        refs["sin"][...],
        refs["allow"][...],
        refs["n"],
        refs["qkv"],
        refs["prob"],
        refs["o"],
    )
    copy = pair.start(part, theirs, partner())
    copy.wait()
    h = x + (part[...] + theirs[...])
    refs["h"][...] = h
    return h, (h * inverse_norm(h) * gain_e).astype(BF)


FRONT_OUT = (
    ("h", (TOKENS, WIDE), F32),
    ("n", (TOKENS, WIDE), BF),
    ("qkv", (TOKENS, QKV), BF),
    ("prob", (HEADS, TOKENS, TOKENS), F32),
    ("o", (TOKENS, OUT), BF),
    ("onehot", (SLOTS, TOKENS), BF),
    ("weighted", (SLOTS, TOKENS), F32),
)
HELD = [
    pltpu.VMEM((2, WIDE, HIDDEN), BF),
    pltpu.VMEM((2, WIDE, HIDDEN), BF),
    pltpu.VMEM((2, HIDDEN, WIDE), BF),
    pltpu.SemaphoreType.DMA((6,)),
]
BLOCKS = pltpu.VMEM((PEERS, CAP, WIDE), BF)
PLANE = pltpu.VMEM((TOKENS, WIDE), F32)
EACH = pltpu.SemaphoreType.DMA((PEERS,))
PAIRED = pltpu.SemaphoreType.DMA((4,))


def forward_kernel(
    layer, x_ref, w_any, cos, sin, allow, ids, weights, gate, up, down, gate_o, up_o, down_o,
    h, n, qkv, prob, o, onehot, weighted, rows, a, b, out,
    w, w_sem, held_g, held_u, held_d, held_sem, sent, came, back, part0, theirs0, part1, theirs1,
    send0, recv0, send1, recv1, pair_send, pair_recv,
):
    load = pltpu.make_async_copy(w_any, w, w_sem)
    load.start()
    held = (held_g, held_u, held_d)
    loads = expert_weight_copies(layer, (gate, up, down), (gate_o, up_o, down_o), held, held_sem)
    greet_peers()
    pair = Sender(pair_send, pair_recv)
    refs = dict(w=w, cos=cos, sin=sin, allow=allow, h=h, n=n, qkv=qkv, prob=prob, o=o)
    hot, heavy = slot_matrices(ids[...], weights[...])
    onehot[...] = hot.astype(BF)
    weighted[...] = heavy
    load.wait()
    x = x_ref[...].astype(F32)
    _, m = attention_part(x, refs, part0, theirs0, pair)
    store_rows(sent, dot(onehot[...], m))
    exchange_start(sent, came, send0, recv0)
    for copy in loads:
        copy.wait()
    exchange_wait(sent, came, send0, recv0)
    rows[...] = rows_of(came)
    store_rows(sent, expert_forward(rows[...], held, a, b))
    exchange_start(sent, back, send1, recv1)
    exchange_wait(sent, back, send1, recv1)
    part1[...] = combine(weighted[...], rows_of(back))
    pair.start(part1, theirs1, partner()).wait()
    out[...] = h[...] + (part1[...] + theirs1[...])


def middle_kernel(
    layer, x_ref, cot, w_any, cos, sin, allow, ids, weights, gate, up, down, gate_o, up_o, down_o,
    h, n, qkv, prob, o, onehot, weighted, y_rows, m_back, grads,
    w, w_sem, held_g, held_u, held_d, held_sem, sent, came, sent_g, came_g, part0, theirs0,
    rows, dy, a, b, z, d, send0, recv0, send1, recv1, pair_send, pair_recv,
):
    load = pltpu.make_async_copy(w_any, w, w_sem)
    load.start()
    held = (held_g, held_u, held_d)
    loads = expert_weight_copies(layer, (gate, up, down), (gate_o, up_o, down_o), held, held_sem)
    greet_peers()
    pair = Sender(pair_send, pair_recv)
    refs = dict(w=w, cos=cos, sin=sin, allow=allow, h=h, n=n, qkv=qkv, prob=prob, o=o)
    hot, heavy = slot_matrices(ids[...], weights[...])
    onehot[...] = hot.astype(BF)
    weighted[...] = heavy
    slot_weight = jnp.sum(heavy, axis=1, keepdims=True)
    store_rows(sent_g, dot(onehot[...], cot[...]) * slot_weight)
    exchange_start(sent_g, came_g, send1, recv1)
    load.wait()
    _, m = attention_part(x_ref[...], refs, part0, theirs0, pair)
    store_rows(sent, dot(onehot[...], m))
    exchange_start(sent, came, send0, recv0)
    for copy in loads:
        copy.wait()
    exchange_wait(sent_g, came_g, send1, recv1)
    dy[...] = rows_of(came_g)
    exchange_wait(sent, came, send0, recv0)
    rows[...] = rows_of(came)
    store_rows(y_rows, expert_forward(rows[...], held, a, b))
    store_rows(m_back, expert_backward(dy[...], held, a, b, z, d))
    expert_gradients(rows, dy, z, d, grads)


def expert_kernel(
    layer, g_ref, onehot, weighted, rows, a, b, gate, up, down, gate_o, up_o, down_o,
    m_back, grads,
    held_g, held_u, held_d, held_sem, sent, came, dy, z, d, send0, recv0,
):
    held = (held_g, held_u, held_d)
    loads = expert_weight_copies(layer, (gate, up, down), (gate_o, up_o, down_o), held, held_sem)
    slot_weight = jnp.sum(weighted[...], axis=1, keepdims=True)
    high, low = halves(g_ref[...])
    store_rows(sent, (dot(onehot[...], high) + dot(onehot[...], low)) * slot_weight)
    greet([peer(s) for s in range(1, PEERS)])
    exchange_start(sent, came, send0, recv0)
    for copy in loads:
        copy.wait()
    exchange_wait(sent, came, send0, recv0)
    dy[...] = rows_of(came)
    store_rows(m_back, expert_backward(dy[...], held, a, b, z, d))
    expert_gradients(rows, dy, z, d, grads)


def back_kernel(
    last, x_ref, g_ref, w_any, cos, sin, h, n, qkv, prob, o, onehot, weighted, m_back, y_rows,
    out, w_grad, block_out,
    w, w_sem, came, back, part0, theirs0, part1, theirs1, part2, theirs2, lin,
    send0, recv0, send1, recv1, pair_send, pair_recv,
):
    load = pltpu.make_async_copy(w_any, w, w_sem)
    load.start()
    greet_peers()
    pair = Sender(pair_send, pair_recv)
    core = lax.axis_index("blk")
    exchange_start(m_back, came, send0, recv0)
    if last:
        exchange_start(y_rows, back, send1, recv1)
    load.wait()
    gain_a, gain_e = gain_rows(w)
    exchange_wait(m_back, came, send0, recv0)
    part0[...] = dot(onehot[...], rows_of(came), 0, 0)
    pair.start(part0, theirs0, partner()).wait()
    dm = part0[...] + theirs0[...]
    hidden = h[...]
    inward, gain_grad_e = norm_back(hidden, inverse_norm(hidden), gain_e, dm)
    gh = g_ref[...].astype(F32) + inward
    out[...] = gh
    da = gh.astype(BF)
    w_grad[:, QKV : QKV + OUT] = dot(da, o[...], 0, 0).astype(BF)
    do = dot(da, w[:, QKV : QKV + OUT]).astype(BF)
    key = qkv[:, HEADS * HEAD : (HEADS + 1) * HEAD]
    value = qkv[:, (HEADS + 1) * HEAD :]
    scale = HEAD ** (-0.5)
    key_grad, value_grad = None, None
    cosine, sine = cos[...], sin[...]
    for i in range(HEADS):
        prob_i = prob[i]
        do_i = head_of(do, i)
        q_i = qkv[:, i * HEAD : (i + 1) * HEAD]
        dprob = dot(do_i, value, 1, 1)
        centre = jnp.sum(prob_i * dprob, axis=-1, keepdims=True)
        ds = (prob_i * (dprob - centre)).astype(BF)
        dq = dot(ds, key) * scale
        lin[:, i * HEAD : (i + 1) * HEAD] = unrotate(dq, cosine, sine).astype(BF)
        dk = dot(ds, q_i, 0, 0)
        dv = dot(prob_i.astype(BF), do_i, 0, 0)
        key_grad = dk if key_grad is None else key_grad + dk
        value_grad = dv if value_grad is None else value_grad + dv
    lin[:, HEADS * HEAD : (HEADS + 1) * HEAD] = unrotate(key_grad * scale, cosine, sine).astype(BF)
    lin[:, (HEADS + 1) * HEAD :] = value_grad.astype(BF)
    part1[...] = dot(lin[...], w[:, 0:QKV], 1, 1)
    across = pair.start(part1, theirs1, partner())
    w_grad[:, 0:QKV] = dot(n[...], lin[...], 0, 0).astype(BF)
    if last:
        exchange_wait(y_rows, back, send1, recv1)
        mixed = combine(weighted[...], rows_of(back))
        theirs_first = core == 1
        part2[...] = jnp.where(theirs_first, mixed[:, :HALF], mixed[:, HALF:])
        second = pair.start(part2, theirs2, partner())
        own = jnp.where(theirs_first, mixed[:, HALF:], mixed[:, :HALF])
        kept = jnp.where(theirs_first, h[:, HALF:], h[:, :HALF])
        second.wait()
        block_out[...] = (kept + (own + theirs2[...])).astype(BF)
    else:
        block_out[...] = jnp.zeros(block_out.shape, BF)
    across.wait()
    dn = part1[...] + theirs1[...]
    x = x_ref[...].astype(F32)
    inward, gain_grad_a = norm_back(x, inverse_norm(x), gain_a, dn)
    out[...] = out[...] + inward
    lane = lax.broadcasted_iota(jnp.int32, (TOKENS, 128), 1)
    total = jnp.zeros((WIDE, 128), F32)
    for i, grad in enumerate((gain_grad_a, gain_grad_e)):
        pick = jnp.where(lane == i, 1.0, 0.0).astype(BF)
        for piece in halves(grad):
            total = total + dot(piece, pick, 0, 0)
    w_grad[:, QKV + OUT :] = total.astype(BF)


def ring_start(sender, block, near, relay, plus, minus):
    relays = [
        sender.start(block(2, 0), relay(0), plus),
        sender.start(block(2, 1), relay(1), minus),
    ]
    plain = [
        sender.start(block(1, 1), near(0, 1), plus),
        sender.start(block(3, 0), near(1, 0), minus),
    ]
    return relays, plain


def ring_relay(sender, block, near, relay, plus, minus, relays):
    sums = []
    for side, (by, target) in enumerate(((1, plus), (3, minus))):
        relays[side].wait_recv()
        held = relay(side)
        held[...] = (block(by, side)[...].astype(F32) + held[...].astype(F32)).astype(BF)
        sums.append(sender.start(held, near(side, side), target))
    return sums


def rings(sender, stages):
    begun = [ring_start(sender, *stage) for stage in stages]
    sums = [ring_relay(sender, *stage, relays) for stage, (relays, _) in zip(stages, begun)]
    for (relays, plain), added in zip(begun, sums):
        for copy in plain + added:
            copy.wait()
        for copy in relays:
            copy.wait_send()


def scatter_kernel(
    grad0, grad1, out0, out1, near1, relay1, sum1, near2, relay2, sum2, near3, send, recv
):
    xyz, core = coords(), lax.axis_index("blk")
    greet([device_at(shifted(xyz, axis, by), core) for axis in range(3) for by in (1, 2, 3)])
    sender = Sender(send, recv)
    grads, outs = (grad0, grad1), (out0, out1)
    jobs = [(l, p) for l in range(LAYERS) for p in range(3)]
    sides = [
        [device_at(shifted(xyz, axis, by), core) for by in (1, 3)] for axis in range(3)
    ]

    def first(l, p):
        axis, split = ORDERS[p][0], ORDERS[p][1]
        left = [a for a in range(3) if a != axis]
        lanes = pl.ds(p * PART, PART)

        def block(by, half):
            index = [pl.ds(0, 4)] * 3
            index[axis] = shifted(xyz, axis, by)[axis]
            if half is not None:
                index[split] = pl.ds(2 * half, 2)
            return grads[l].at[index[0], index[1], index[2], :, lanes]

        def near(side, half):
            index = [pl.ds(2 * half, 2) if a == split else pl.ds(0, 4) for a in left]
            return near1.at[l, p, side, index[0], index[1]]

        def relay(side):
            index = [pl.ds(0, 2) if a == split else pl.ds(0, 4) for a in left]
            return relay1.at[l, p, side, index[0], index[1]]

        return block, near, relay, *sides[axis]

    def second(l, p):
        axis, split = ORDERS[p][1], ORDERS[p][2]
        left = [a for a in range(3) if a != ORDERS[p][0]]

        def block(by, half):
            rest = pl.ds(0, 4) if half is None else pl.ds(2 * half, 2)
            index = [shifted(xyz, axis, by)[axis] if a == axis else rest for a in left]
            return sum1.at[l, p, index[0], index[1]]

        def near(side, half):
            return near2.at[l, p, side, pl.ds(2 * half, 2)]

        def relay(side):
            return relay2.at[l, p, side]

        return block, near, relay, *sides[axis]

    rings(sender, [first(l, p) for l, p in jobs])
    for l, p in jobs:
        mine = first(l, p)[0](0, None)
        sum1[l, p] = (
            mine[...].astype(F32) + near1[l, p, 0].astype(F32) + near1[l, p, 1].astype(F32)
        ).astype(BF)
    rings(sender, [second(l, p) for l, p in jobs])
    for l, p in jobs:
        mine = second(l, p)[0](0, None)
        sum2[l, p] = (
            mine[...].astype(F32) + near2[l, p, 0].astype(F32) + near2[l, p, 1].astype(F32)
        ).astype(BF)
    copies = []
    for l, p in jobs:
        axis = ORDERS[p][2]
        for by in (1, 3, 2):
            there = shifted(xyz, axis, by)
            copies.append(
                sender.start(sum2.at[l, p, there[axis]], near3.at[l, p, by - 1], device_at(there, core))
            )
    for copy in copies:
        copy.wait()
    for l, p in jobs:
        total = sum2[l, p, xyz[ORDERS[p][2]]].astype(F32)
        for side in range(3):
            total = total + near3[l, p, side].astype(F32)
        outs[l][:, p * PART : (p + 1) * PART] = total


def kernel_call(kernel, cid, outs, scratch, operands):
    return pl.pallas_call(
        kernel,
        out_shape=[jax.ShapeDtypeStruct(o[0], o[1]) for o in outs],
        in_specs=[ANY if stays else VMEM for _, stays in operands],
        out_specs=[ANY if o[2] else VMEM for o in outs],
        scratch_shapes=scratch,
        compiler_params=pltpu.CompilerParams(
            collective_id=cid, has_side_effects=True, vmem_limit_bytes=LIMIT
        ),
    )(*[array for array, _ in operands])


def sems(*counts):
    return [pltpu.SemaphoreType.DMA((n,)) for n in counts]


def positions(lengths, row_count):
    seq_ends = jnp.cumsum(lengths)
    starts = seq_ends - lengths
    places = jnp.arange(row_count, dtype=jnp.int32)
    segment = jnp.sum((places[:, None] >= seq_ends[None, :]).astype(jnp.int32), axis=1)
    chosen = segment[:, None] == jnp.arange(lengths.shape[0], dtype=jnp.int32)[None, :]
    offset = jnp.sum(jnp.where(chosen, starts[None, :], 0), axis=1)
    return (segment, places - offset)


def rope_tables(places):
    half_dim = HEAD // 2
    frequency = rope_base ** (-2.0 * jnp.arange(half_dim, dtype=F32) / HEAD)
    angles = places.astype(F32)[:, None] * frequency[None, :]
    cos, sin = jnp.cos(angles), jnp.sin(angles)
    return jnp.concatenate([cos, cos], axis=-1), jnp.concatenate([-sin, sin], axis=-1)


def per_device(
    tokens_in,
    seq_lengths,
    expert_ids,
    gate_weights,
    attention_gain,
    query_weight,
    key_weight,
    value_weight,
    out_weight,
    expert_gain,
    gate_weight,
    up_weight,
    down_weight,
    cotangent,
):
    core = lax.axis_index("blk")
    gains = jnp.stack([attention_gain, expert_gain], axis=-1)
    shard = jnp.concatenate(
        [
            query_weight,
            key_weight,
            value_weight,
            jnp.swapaxes(out_weight, 1, 2),
            jnp.pad(gains, ((0, 0), (0, 0), (0, 126))),
        ],
        axis=2,
    )
    cube = (4, 4, 4, SHARD, COLS)
    w0, w1, tokens, cot, gate_o, up_o, down_o = kernel_call(
        gather_kernel,
        1,
        [
            (cube, BF, True),
            (cube, BF, True),
            ((TOKENS, WIDE), BF, False),
            ((TOKENS, WIDE), BF, False),
            ((LAYERS, WIDE, HIDDEN), BF, True),
            ((LAYERS, WIDE, HIDDEN), BF, True),
            ((LAYERS, HIDDEN, WIDE), BF, True),
        ],
        sems(80, 80, 4),
        [
            (shard, False),
            (tokens_in, False),
            (cotangent, False),
            (gate_weight, True),
            (up_weight, True),
            (down_weight, True),
        ],
    )
    whole = [w.reshape(WIDE, COLS) for w in (w0, w1)]
    experts = [(a, True) for a in (gate_weight, up_weight, down_weight, gate_o, up_o, down_o)]
    segment, places = positions(seq_lengths[0], TOKENS)
    cos, sin = rope_tables(places)
    allow = (segment[:, None] == segment[None, :]) & (places[None, :] <= places[:, None])
    tables = [(cos, False), (sin, False), (allow.astype(F32), False)]
    slots = [
        [(expert_ids[l].T, False), (gate_weights[l].T, False)] for l in range(LAYERS)
    ]
    front = [(shape, kind, False) for _, shape, kind in FRONT_OUT]
    names = [name for name, _, _ in FRONT_OUT]
    inner = ((2, SLOTS, HIDDEN), F32, False)
    block = ((PEERS, CAP, WIDE), BF, False)
    plane = ((TOKENS, WIDE), F32, False)
    grads = ((4, 6, HIDDEN, HIDDEN), BF, False)
    load = [pltpu.VMEM((WIDE, COLS), BF), pltpu.SemaphoreType.DMA]
    rows_in = pltpu.VMEM((SLOTS, WIDE), BF)

    *kept0, rows0, a0, b0, stream = kernel_call(
        functools.partial(forward_kernel, 0),
        2,
        front + [((SLOTS, WIDE), BF, False), inner, inner, plane],
        load
        + HELD
        + [BLOCKS] * 3
        + [PLANE] * 4
        + sems(PEERS, PEERS, PEERS, PEERS, 4, 4),
        [(tokens, False), (whole[0], True)] + tables + slots[0] + experts,
    )
    kept0 = dict(zip(names, kept0))
    *kept1, y_rows, m_back1, grads1 = kernel_call(
        functools.partial(middle_kernel, 1),
        3,
        front + [block, block, grads],
        load
        + HELD
        + [BLOCKS] * 4
        + [PLANE] * 2
        + [rows_in, rows_in]
        + [pltpu.VMEM((2, SLOTS, HIDDEN), F32)] * 2
        + [pltpu.VMEM((SLOTS, 2 * HIDDEN), BF), pltpu.VMEM((SLOTS, 4 * HIDDEN), BF)]
        + sems(PEERS, PEERS, PEERS, PEERS, 4, 4),
        [(stream, False), (cot, False), (whole[1], True)] + tables + slots[1] + experts,
    )
    kept1 = dict(zip(names, kept1))

    def back(last, cid, x, upstream, w, kept, m_back, y_rows):
        fields = ("h", "n", "qkv", "prob", "o", "onehot", "weighted")
        return kernel_call(
            functools.partial(back_kernel, last),
            cid,
            [plane, ((WIDE, COLS), BF, False), ((TOKENS, HALF), BF, False)],
            load
            + [BLOCKS] * 2
            + [PLANE] * 4
            + [pltpu.VMEM((TOKENS, HALF), F32)] * 2
            + [pltpu.VMEM((TOKENS, QKV), BF)]
            + sems(PEERS, PEERS, PEERS, PEERS, 4, 4),
            [(x, False), (upstream, False), (w, True)]
            + tables[:2]
            + [(kept[f], False) for f in fields]
            + [(m_back, False), (y_rows, False)],
        )

    def summed(grads):
        total = lax.psum_scatter(grads, "dp", scatter_dimension=0, tiled=True)[0]
        theirs = lax.ppermute(total[3:], "blk", [(0, 1), (1, 0)])
        first = jnp.where(core == 0, total[:3], theirs).astype(F32)
        second = jnp.where(core == 0, theirs, total[:3]).astype(F32)
        return [jnp.stack([first[i], second[i]]) for i in range(3)]

    expert1 = summed(grads1)
    upstream, w_grad1, block_out = back(
        True, 4, stream, cot, whole[1], kept1, m_back1, y_rows
    )
    m_back0, grads0 = kernel_call(
        functools.partial(expert_kernel, 0),
        5,
        [block, grads],
        HELD
        + [BLOCKS] * 2
        + [rows_in]
        + [pltpu.VMEM((SLOTS, 2 * HIDDEN), BF), pltpu.VMEM((SLOTS, 4 * HIDDEN), BF)]
        + sems(PEERS, PEERS),
        [(upstream, False), (kept0["onehot"], False), (kept0["weighted"], False)]
        + [(rows0, False), (a0, False), (b0, False)]
        + experts,
    )
    expert0 = summed(grads0)
    upstream, w_grad0, _ = back(False, 6, tokens, upstream, whole[0], kept0, m_back0, m_back0)
    ring = (LAYERS, 3, 2, 4, 4, SHARD, PART)
    att0, att1 = kernel_call(
        scatter_kernel,
        7,
        [((SHARD, COLS), F32, False)] * 2,
        [
            pltpu.VMEM(ring, BF),
            pltpu.VMEM(ring, BF),
            pltpu.VMEM((LAYERS, 3, 4, 4, SHARD, PART), BF),
            pltpu.VMEM((LAYERS, 3, 2, 4, SHARD, PART), BF),
            pltpu.VMEM((LAYERS, 3, 2, 2, SHARD, PART), BF),
            pltpu.VMEM((LAYERS, 3, 4, SHARD, PART), BF),
            pltpu.VMEM((LAYERS, 3, 3, SHARD, PART), BF),
        ]
        + sems(90, 90),
        [(w_grad0.reshape(cube), False), (w_grad1.reshape(cube), False)],
    )
    att = jnp.stack([att0, att1])
    grad_tokens = lax.dynamic_slice_in_dim(upstream, core * HALF, HALF, 1)
    return (
        block_out,
        grad_tokens,
        att[:, :, QKV + OUT],
        att[:, :, :768],
        att[:, :, 768:896],
        att[:, :, 896:QKV],
        jnp.swapaxes(att[:, :, QKV : QKV + OUT], 1, 2),
        att[:, :, QKV + OUT + 1],
        *[jnp.stack([first, second]) for first, second in zip(expert0, expert1)],
    )


def solution(mesh):
    placed = (
        P(("dp", "expert"), "blk"),
        P(("dp", "expert"), None),
        P(None, ("dp", "expert"), None),
        P(None, ("dp", "expert"), None),
        P(None, ("dp", "expert")),
        P(None, ("dp", "expert"), "blk"),
        P(None, ("dp", "expert"), "blk"),
        P(None, ("dp", "expert"), "blk"),
        P(None, "blk", ("dp", "expert")),
        P(None, ("dp", "expert")),
        P(None, "expert", None, "blk"),
        P(None, "expert", None, "blk"),
        P(None, "expert", "blk", None),
        P(("dp", "expert"), "blk"),
    )
    return jax.shard_map(
        per_device,
        mesh=mesh,
        in_specs=placed,
        out_specs=(
            P(("dp", "expert"), "blk"),
            P(("dp", "expert"), "blk"),
            P(None, ("dp", "expert")),
            P(None, ("dp", "expert"), "blk"),
            P(None, ("dp", "expert"), "blk"),
            P(None, ("dp", "expert"), "blk"),
            P(None, "blk", ("dp", "expert")),
            P(None, ("dp", "expert")),
            P(None, "expert", "dp", "blk"),
            P(None, "expert", "dp", "blk"),
            P(None, "expert", "blk", "dp"),
        ),
        check_vma=False,
    )
```

time: 1130 us -> 510 us (0.45)
  blocking collectives: 468 us -> 0 us
  Pallas kernels: 0 us -> 382 us
  local copies, waits for them, and re-layouts: 230 us -> 13.4 us
  waiting for transfers between devices: 191 us -> 75.9 us
  other arithmetic: 92.5 us -> 13.9 us
  matrix products: 76.7 us -> 0 us
  starting transfers between devices: 34.6 us -> 0.25 us
    pallas_call x0 -> x7, Pallas kernels: none -> 382 us  [kernel_call(): pl.pallas_call(kernel, out_shape=[jax.ShapeDtypeStruct(o[0], o[1]) for o...]
    unnamed x1 -> x0, blocking collectives: 348 us -> none
    all_to_all x14 -> x0, blocking collectives: 120 us -> none  [the longest x8 42.2 us: copy_for_each(): return lax.all_to_all(copies, axis, split_axis=0, concat_axis=0, tiled=True)]
    all_gather x6 -> x0, waiting for transfers between devices: 102 us -> none  [the longest x2 94.8 us: gather_turned(): lax.all_gather(both, axis, axis=0, tiled=True)]
    all_to_all x8 -> x0, waiting for transfers between devices: 89.5 us -> none  [the longest x2 37 us: per_device(): lax.all_to_all(row_grad, 'expert', split_axis=0, concat_axis=0, tiled=True)]
    dot_general x54 -> x0, matrix products: 76.7 us -> none  [the longest x2 6.98 us: per_device(): jnp.dot(mixed_heads, out_full, preferred_element_type=jnp.float32)]
    reduce_scatter x1 -> x2, waiting for transfers between devices: 0.01 us -> 73.3 us  [summed(): total = lax.psum_scatter(grads, 'dp', scatter_dimension=0, tiled=True)[0]]
    concatenate x4 -> x0, local copies, waits for them, and re-layouts: 58.4 us -> none  [the longest x2 56.9 us: sent_together(): both = jnp.concatenate(columns, axis=along)]
  transfers between devices with their start and end apart: 17 -> 4, of which waited for: 8 -> 2; matrix products, arithmetic and copies ran while one was open for 24% -> 2% of each run, Pallas kernels for 0% -> 25%
where the time goes in v1:
time: 510 us; the launch traced here: 500 us
  Pallas kernels  382 us (75%)
  waiting for transfers between devices  75.9 us (15%)
  between operations  14.5 us (3%)
  other arithmetic  13.9 us (3%)
  local copies, waits for them, and re-layouts  13.4 us (3%)
    pallas_call x7, Pallas kernels, kernel_call(): pl.pallas_call(kernel, out_shape=[jax.ShapeDtypeStruct(o[0], o[1]) for o...  382 us
    reduce_scatter x2, waiting for transfers between devices, summed(): total = lax.psum_scatter(grads, 'dp', scatter_dimension=0, tiled=True)[0]  73.3 us
  transfers between devices with their start and end apart: 4, of which 2 were waited for; matrix products, arithmetic and copies ran while one was open for 2% of the time, Pallas kernels for 25%

profile of v1, /device:TPU:0, one launch (start us, length us, event | category | flops | bytes accessed | tf_op | source)
XLA Modules:
  0.0 500.4 jit_solution(4687364633412216741)
XLA Ops:
  7.2 0.0 reduce-scatter.3.cloned.1.call-start
  7.2 0.8 reduce-window.4
  8.1 0.7 fusion.11
  8.7 0.1 convert_reduce_fusion
  8.8 0.1 select_reduce_fusion
  8.9 0.9 constant_dynamic-update-slice_fusion.2
  9.8 0.8 copy.32
  10.5 0.8 copy.33
  11.3 0.7 and_convert_fusion.allow
  12.0 1.3 slice_bitcast_fusion.4
  13.3 1.3 slice_bitcast_fusion.5
  14.6 0.3 fusion.8
  14.9 0.7 constant_dynamic-update-slice_fusion.1
  15.6 0.7 constant_dynamic-update-slice_fusion
  16.3 0.9 bitcast_dynamic-update-slice_fusion
  17.2 0.8 pad_maximum_fusion.3
  18.0 0.1 fusion.10.shard
  18.1 0.0 copy-start.2
  18.1 0.7 copy-done.2
  18.7 58.9 %shard_map.221 = (bf16[4,4,4,24,1920]{4,3,2,1,0:T(8,128)(2,1)}, bf16[4,4,4,24,1920]{4,3,2,1,0:T(8,128)(2,1)}, bf16[128,1536]{1,0:T(8,128)(2,1)}, bf16[128,1536]{...) custom-call(bf16[2,24,1920]{2,1,0:T(8,128)(2,1)} %copy-done.2, ...), custom_call_target="tpu_custom_call" | custom-call | tf_op jit(solution)/shard_map/pallas_call | solution.py:671
  77.7 61.7 %shard_map.222 = (f32[128,1536]{1,0:T(8,128)}, bf16[128,1536]{1,0:T(8,128)(2,1)}, bf16[128,1024]{1,0:T(8,128)(2,1)}, f32[6,128,128]{2,1,0:T(8,128)}, bf16[128,76...) custom-call(bf16[128,1536]{1,0:T(8,128)(2,1)} %get-tuple-element.48., ...), custom_call_target="tpu_custom_call" | custom-call | tf_op jit(solution)/shard_map/pallas_call | solution.py:671
  139.4 55.7 %shard_map.223 = (f32[128,1536]{1,0:T(8,128)}, bf16[128,1536]{1,0:T(8,128)(2,1)}, bf16[128,1024]{1,0:T(8,128)(2,1)}, f32[6,128,128]{2,1,0:T(8,128)}, bf16[128,76...) custom-call(f32[128,1536]{1,0:T(8,128)} %get-tuple-element.53.x_ref,, ...), custom_call_target="tpu_custom_call" | custom-call | tf_op jit(solution)/shard_map/pallas_call | solution.py:671
  195.1 42.4 %shard_map.224 = (f32[128,1536]{1,0:T(8,128)}, bf16[1536,1920]{1,0:T(8,128)(2,1)}, bf16[128,768]{1,0:T(8,128)(2,1)}) custom-call(f32[128,1536]{1,0:T(8,128)} %get-tuple-element.53.x_ref, bf16[128,1536]{1,0:T(8,128)(2,1)} %get-tuple-element.54.cot.g_ref, bf16[1536,1920]{1,0:T(8,128)(2,1)} %bitcast.67, f32[128,128]{1,0:T(8,128)} %get-tuple-element.116.cos, ...), custom_call_target="tpu_custom_call" | custom-call | tf_op jit(solution)/shard_map/pallas_call | solution.py:671
  237.5 41.1 %shard_map.225 = (bf16[16,24,1536]{2,1,0:T(8,128)(2,1)}, bf16[4,6,384,384]{3,2,1,0:T(8,128)(2,1)}) custom-call(f32[128,1536]{1,0:T(8,128)} %get-tuple-element.66.g_ref, bf16[384,128]{1,0:T(8,128)(2,1)} %get-tuple-element.72.onehot, f32[384,128]{1,0:T(8,128)} %get-tuple-element.73.weighted, bf16[384,1536]{1,0:T(8,128)(2,1)} %get-tuple-element.74.rows, ...), custom_call_target="tpu_custom_call" | custom-call | tf_op jit(solution)/shard_map/pallas_call | solution.py:671
  278.6 0.0 reduce-scatter.3.cloned.1.call-update
  278.6 0.0 reduce-scatter.5.cloned.1.call-start
  278.7 0.7 reduce-scatter.5.cloned.1.call-update
  279.4 73.3 %reduce-scatter.3.cloned.1.call-done = bf16[1,6,384,384]{3,2,1,0:T(8,128)(2,1)} async-done(((bf16[4,6,384,384]{3,2,1,0:T(8,128)(2,1)}), bf16[1,6,384,384]{3,2,1,0:T(8,128)(2,1)}) %reduce-scatter.3.cloned.1.call-update) | async-done | bytes 1769488 | tf_op jit(solution)/shard_map/reduce_scatter | solution.py:821
  352.7 1.3 slice_bitcast_fusion.2
  353.9 0.1 collective-permute-start
  354.0 37.9 %shard_map.226 = (f32[128,1536]{1,0:T(8,128)}, bf16[1536,1920]{1,0:T(8,128)(2,1)}, bf16[128,768]{1,0:T(8,128)(2,1)}) custom-call(bf16[128,1536]{1,0:T(8,128)(2,1)} %get-tuple-element.48.x_ref, f32[128,1536]{1,0:T(8,128)} %get-tuple-element.66.g_ref, bf16[1536,1920]{1,0:T(8,128)(2,1)} %bitcast.65, f32[128,128]{1,0:T(8,128)} %get-tuple-element.116.cos, ...), custom_call_target="tpu_custom_call" | custom-call | tf_op jit(solution)/shard_map/pallas_call | solution.py:671
  392.0 84.7 %shard_map.227 = (f32[24,1920]{1,0:T(8,128)}, f32[24,1920]{1,0:T(8,128)}) custom-call(bf16[4,4,4,24,1920]{4,3,2,1,0:T(8,128)(2,1)} %bitcast.69, bf16[4,4,4,24,1920]{4,3,2,1,0:T(8,128)(2,1)} %bitcast.68), custom_call_target="tpu_custom_call" | custom-call | tf_op jit(solution)/shard_map/pallas_call | solution.py:671
  476.7 1.5 fusion.5
  478.2 0.0 copy-start.1
  478.2 1.5 fusion.4
  479.7 1.7 fusion.1
  481.4 1.8 constant_dynamic-slice_fusion
  483.2 0.0 reduce-scatter.5.cloned.1.call-done
  483.2 1.3 slice_bitcast_fusion
  484.4 0.1 collective-permute-start.1
  484.5 0.0 collective-permute-done
  484.5 0.0 copy-done.1
  484.6 0.2 select_convert_fusion.3
  484.8 0.1 fusion.13
  484.9 0.0 copy-start
  484.9 0.1 fusion.14
  485.1 1.9 collective-permute-done.1
  486.9 0.0 copy-done
  486.9 0.2 select_convert_fusion.1
  487.2 0.1 fusion.16
  487.3 0.1 fusion.15
  487.4 0.1 maximum_bitcast_fusion.4
  487.5 0.1 maximum_bitcast_fusion.5
  487.6 1.6 pad_maximum_fusion.2
  489.2 0.1 maximum_bitcast_fusion.2
  489.2 0.1 maximum_bitcast_fusion.3
  489.3 1.6 pad_maximum_fusion.1
  490.9 0.1 maximum_bitcast_fusion
  491.0 0.1 maximum_bitcast_fusion.1
  491.1 0.0 copy-start.3
  491.1 1.6 pad_maximum_fusion
  492.7 0.0 copy-done.3
  492.7 0.7 copy.39
  (2 shorter events, 0.0 us)
Async XLA Ops:
  7.2 345.5 %reduce-scatter.3.cloned.1.call-start = ((), (), s32[]{:S(2)}) async-start(), calls=%async_computation.2 | async-start | bytes 8847360 | tf_op jit(solution)/shard_map/reduce_scatter | solution.py:821
  18.1 0.7 copy-start.2
  278.6 204.5 %reduce-scatter.5.cloned.1.call-start = ((), (), s32[]{:S(2)}) async-start(), calls=%async_computation.3 | async-start | bytes 8847360 | tf_op jit(solution)/shard_map/reduce_scatter | solution.py:821
  353.9 130.6 %collective-permute-start = (bf16[3,384,384]{2,1,0:T(8,128)(2,1)S(1)}, bf16[3,384,384]{2,1,0:T(8,128)(2,1)S(1)}, u32[]{:S(2)}, u32[]{:S(2)}) collective-permute-start(bf16[3,384,384]{2,1,0:T(8,128)(2,1)S(1)} %slice_bitcast_fusion.2), channel_id=1, source_target_pairs={{0,1},{1,0},{2,3},{3,2},{4,5},{5,4},{6,7},{7,6},{8,9},{9,8},{10,11... | collective-permute-start | bytes 2654216 | tf_op jit(solution)/shard_map/ppermute | solution.py:822
  478.2 6.4 %copy-start.1 = (bf16[1,6,384,384]{3,2,1,0:T(8,128)(2,1)S(1)}, bf16[1,6,384,384]{3,2,1,0:T(8,128)(2,1)}, u32[]{:S(2)}) copy-start(bf16[1,6,384,384]{3,2,1,0:T(8,128)(2,1)} %reduce-scatter.3.cloned.1.call-done) | copy-start | bytes 5308420
  484.4 2.5 collective-permute-start.1
  484.9 2.0 copy-start
  491.1 1.6 copy-start.3
Sparse Core Ops, SparseCore 0:
  278.8 73.8 reduce-scatter.2
  355.1 88.6 reduce-scatter.4

commit v2 on v1

v2 whole, which is shorter than its diff:
```python
import functools
import math
import types

import jax
import jax.numpy as jnp
from jax import lax
from jax.experimental import pallas as pl
from jax.experimental.pallas import tpu as pltpu
from jax.sharding import PartitionSpec as P

HEAD = 128
TOP = 4
LAYERS = 2
F32 = jnp.float32
BF = jnp.bfloat16
MESH = pl.DeviceIdType.MESH

epsilon = 1e-06
rope_base = 1000000.0

TOKENS = 128
WIDE = 1536
HALF = WIDE // 2
HEADS = 6
HIDDEN = 384
PEERS = 16
CAP = 24
SLOTS = PEERS * CAP
SHARD = 24
QKV = 1024
OUT = 768
COLS = QKV + OUT + 128
PART = COLS // 3
ORDERS = ((0, 1, 2), (1, 2, 0), (2, 0, 1))
LIMIT = 60 << 20
LATER = ((0, 640, (1, 2, 0)), (640, 640, (2, 1, 0)), (1280, 384, (0, 2, 1)), (1664, 256, (0, 1, 2)))

ANY = pl.BlockSpec(memory_space=pl.ANY)
VMEM = pl.BlockSpec(memory_space=pltpu.VMEM)
SMEM = pl.BlockSpec(memory_space=pltpu.SMEM)


def dot(a, b, ca=1, cb=0):
    return lax.dot_general(a, b, (((ca,), (cb,)), ((), ())), preferred_element_type=F32)


def coords():
    ex = lax.axis_index("expert")
    return [lax.axis_index("dp"), lax.div(ex, 4), lax.rem(ex, 4)]


def shifted(xyz, axis, by):
    moved = list(xyz)
    moved[axis] = lax.rem(xyz[axis] + by, 4)
    return moved


def device_at(xyz, core):
    return (xyz[0], xyz[1] * 4 + xyz[2], core)


def partner():
    return (lax.axis_index("dp"), lax.axis_index("expert"), 1 - lax.axis_index("blk"))


def hail(devices):
    barrier = pltpu.get_barrier_semaphore()
    for device in devices:
        pl.semaphore_signal(barrier, inc=1, device_id=device, device_id_type=MESH)
    return len(devices)


def heard(count):
    pl.semaphore_wait(pltpu.get_barrier_semaphore(), count)


def peer(step):
    dp, ex, core = (lax.axis_index(a) for a in ("dp", "expert", "blk"))
    return (dp, lax.rem(ex + step, PEERS), core)


def peers():
    return [peer(d) for d in range(1, PEERS)] + [partner()]


class Local:
    def __init__(self, sem):
        self.sem, self.at, self.kept = sem, 0, []

    def start(self, src, dst):
        assert self.at < self.sem.shape[0]
        copy = pltpu.make_async_copy(src, dst, self.sem.at[self.at])
        self.at += 1
        copy.start()
        return copy

    def keep(self, src, dst):
        self.kept.append(self.start(src, dst))

    def wait_kept(self):
        for copy in self.kept:
            copy.wait()


class Sender:
    def __init__(self, send, recv):
        self.send, self.recv, self.at = send, recv, 0

    def start(self, src, dst, device):
        assert self.at < self.send.shape[0]
        copy = pltpu.make_async_remote_copy(
            src_ref=src,
            dst_ref=dst,
            send_sem=self.send.at[self.at],
            recv_sem=self.recv.at[self.at],
            device_id=device,
            device_id_type=MESH,
        )
        self.at += 1
        copy.start()
        return copy


def exchange_copy(src, dst, send, recv, step):
    me = lax.axis_index("expert")
    target = peer(step)
    return pltpu.make_async_remote_copy(
        src_ref=src.at[target[1]],
        dst_ref=dst.at[me],
        send_sem=send.at[step],
        recv_sem=recv.at[step],
        device_id=target,
        device_id_type=MESH,
    )


def exchange_start(src, dst, send, recv):
    me = lax.axis_index("expert")

    def begin(step, carry):
        exchange_copy(src, dst, send, recv, step).start()
        return carry

    lax.fori_loop(1, PEERS, begin, 0)
    pltpu.make_async_copy(src.at[me], dst.at[me], send.at[0]).start()


def exchange_wait(src, dst, send, recv):
    me = lax.axis_index("expert")

    def end(step, carry):
        exchange_copy(src, dst, send, recv, step).wait()
        return carry

    lax.fori_loop(1, PEERS, end, 0)
    pltpu.make_async_copy(src.at[me], dst.at[me], send.at[0]).wait()


def rows_of(ref):
    return ref[...].astype(F32).reshape(SLOTS, WIDE).astype(BF)


def store_rows(ref, rows):
    ref[...] = rows.reshape(PEERS, CAP, WIDE).astype(BF)


def slot_matrices(ids, weights):
    core = lax.axis_index("blk")
    lane = lax.broadcasted_iota(jnp.int32, (TOKENS, 128), 1)
    expert = 2 * lane + core
    chosen = jnp.zeros((TOKENS, 128), F32)
    gate = jnp.zeros((TOKENS, 128), F32)
    for j in range(TOP):
        hit = jnp.where(ids[:, j : j + 1] == expert, 1.0, 0.0)
        chosen = chosen + hit
        gate = gate + hit * weights[:, j : j + 1]
    chosen, gate = chosen.T[:PEERS], gate.T[:PEERS]
    before = lax.broadcasted_iota(jnp.int32, (TOKENS, TOKENS), 0) < lax.broadcasted_iota(
        jnp.int32, (TOKENS, TOKENS), 1
    )
    rank = dot(chosen.astype(BF), jnp.where(before, 1.0, 0.0).astype(BF))
    rank = jnp.where(chosen > 0.0, rank, -1.0)
    shape = (PEERS, CAP, TOKENS)
    place = lax.broadcasted_iota(jnp.int32, shape, 1).astype(F32)
    onehot = jnp.where(jnp.broadcast_to(rank[:, None, :], shape) == place, 1.0, 0.0)
    weighted = onehot * jnp.broadcast_to(gate[:, None, :], shape)
    return onehot.reshape(SLOTS, TOKENS), weighted.reshape(SLOTS, TOKENS)


def halves(value):
    high = value.astype(BF)
    return high, (value - high.astype(F32)).astype(BF)


def combine(weighted, rows):
    high, low = halves(weighted)
    return dot(high, rows, 0, 0) + dot(low, rows, 0, 0)


def gain_rows(w_ref):
    unit = jnp.where(
        lax.broadcasted_iota(jnp.int32, (8, 128), 0) == lax.broadcasted_iota(jnp.int32, (8, 128), 1),
        1.0,
        0.0,
    ).astype(BF)
    rows = dot(unit, w_ref[:, QKV + OUT : COLS], 1, 1)
    return rows[0:1, :], rows[1:2, :]


def inverse_norm(u):
    return lax.rsqrt(jnp.mean(u * u, axis=-1, keepdims=True) + epsilon)


def norm_back(u, inverse, gain, upstream):
    scaled = upstream * gain
    inward = inverse * scaled - u * (inverse * inverse * inverse) * jnp.mean(
        u * scaled, axis=-1, keepdims=True
    )
    return inward, upstream * u * inverse


def rotate(u, cos, sin):
    return u * cos + pltpu.roll(u, HEAD // 2, 1) * sin


def unrotate(u, cos, sin):
    return u * cos - pltpu.roll(u, HEAD // 2, 1) * sin


def head_of(value, h):
    return value[:, h * HEAD : (h + 1) * HEAD]


def attention(x, gain, w_ref, cos, sin, allow, n_ref, qkv_ref, prob_ref, o_ref):
    n = (x * inverse_norm(x) * gain).astype(BF)
    n_ref[...] = n
    flat = dot(n, w_ref[:, 0:QKV])
    for h in range(HEADS + 1):
        qkv_ref[:, h * HEAD : (h + 1) * HEAD] = rotate(head_of(flat, h), cos, sin).astype(BF)
    qkv_ref[:, (HEADS + 1) * HEAD :] = flat[:, (HEADS + 1) * HEAD :].astype(BF)
    key = qkv_ref[:, HEADS * HEAD : (HEADS + 1) * HEAD]
    value = qkv_ref[:, (HEADS + 1) * HEAD :]
    for h in range(HEADS):
        scores = dot(qkv_ref[:, h * HEAD : (h + 1) * HEAD], key, 1, 1) * HEAD ** (-0.5)
        scores = jnp.where(allow > 0.0, scores, -1e30)
        weight = jnp.exp(scores - jnp.max(scores, axis=-1, keepdims=True))
        prob = weight / jnp.sum(weight, axis=-1, keepdims=True)
        prob_ref[h] = prob
        o_ref[:, h * HEAD : (h + 1) * HEAD] = dot(prob.astype(BF), value).astype(BF)
    return dot(o_ref[...], w_ref[:, QKV : QKV + OUT], 1, 1)


def expert_weight_copies(layer, r, local):
    core = lax.axis_index("blk")
    copies = []
    for name in ("gate", "up", "down"):
        held = getattr(r, "held_" + name)
        copies.append(local.start(getattr(r, name).at[layer, core], held.at[0]))
        copies.append(local.start(getattr(r, name + "_other").at[layer], held.at[1]))
    return copies


def expert_forward(rows, held, a_ref, b_ref):
    gate, up, down = held
    total = None
    for c in range(2):
        a = dot(rows, gate[c])
        b = dot(rows, up[c])
        a_ref[c] = a
        b_ref[c] = b
        z = (a / (1.0 + jnp.exp(-a)) * b).astype(BF)
        term = dot(z, down[c])
        total = term if total is None else total + term
    return total


def expert_backward(dy, held, a_ref, b_ref, z_ref, d_ref):
    gate, up, down = held
    total = None
    for c in range(2):
        a = a_ref[c]
        b = b_ref[c]
        sg = 1.0 / (1.0 + jnp.exp(-a))
        z_ref[:, c * HIDDEN : (c + 1) * HIDDEN] = (a * sg * b).astype(BF)
        dz = dot(dy, down[c], 1, 1)
        da = (dz * b * sg * (1.0 + a * (1.0 - sg))).astype(BF)
        db = (dz * a * sg).astype(BF)
        d_ref[:, 2 * c * HIDDEN : (2 * c + 1) * HIDDEN] = da
        d_ref[:, (2 * c + 1) * HIDDEN : (2 * c + 2) * HIDDEN] = db
        term = dot(da, gate[c], 1, 1) + dot(db, up[c], 1, 1)
        total = term if total is None else total + term
    return total


def expert_gradients(rows_ref, dy_ref, z_ref, d_ref, stage, grads, local):
    sent = []
    for q in range(4):
        if q >= 2:
            sent[q - 2].wait()
        columns = slice(q * HIDDEN, (q + 1) * HIDDEN)
        slot = q % 2
        both = dot(rows_ref[:, columns], d_ref[...], 0, 0)
        for c in range(2):
            for i in range(2):
                at = (2 * c + i) * HIDDEN
                stage[slot, 3 * c + i] = both[:, at : at + HIDDEN].astype(BF)
        low = dot(z_ref[...], dy_ref[:, columns], 0, 0)
        for c in range(2):
            stage[slot, 3 * c + 2] = low[c * HIDDEN : (c + 1) * HIDDEN].astype(BF)
        sent.append(local.start(stage.at[slot], grads.at[q]))
    return sent[2:]


def ring_devices(xyz, core, axis, steps=(1, 2, 3)):
    return [device_at(shifted(xyz, axis, by), core) for by in steps]


class Gather:
    def __init__(self, sender, xyz, core):
        self.sender, self.xyz, self.core = sender, xyz, core

    def slab(self, job, stage, at, half=None):
        whole, lane, lanes, order = job
        index = list(at)
        for axis in order[:stage]:
            index[axis] = pl.ds(0, 4)
        if half is not None:
            index[order[0]] = pl.ds(2 * half, 2)
        return whole.at[index[0], index[1], index[2], :, pl.ds(lane, lanes)]

    def to(self, job, stage, by):
        return device_at(shifted(self.xyz, job[3][stage], by), self.core)

    def first(self, job, shard):
        source = shard.at[:, pl.ds(job[1], job[2])]
        target = self.slab(job, 0, self.xyz)
        return [self.sender.start(source, target, self.to(job, 0, by)) for by in (1, 3, 2)]

    def near(self, job, stage):
        block = self.slab(job, stage, self.xyz)
        return [self.sender.start(block, block, self.to(job, stage, by)) for by in (1, 3)]

    def relay(self, job, stage, near):
        copies = []
        for half, by in enumerate((1, 3)):
            near[half].wait_recv()
            at = shifted(self.xyz, job[3][stage], 4 - by)
            block = self.slab(job, stage, at, half)
            copies.append(self.sender.start(block, block, self.to(job, stage, by)))
        return copies

    def finish(self, near, relays):
        for copy in near:
            copy.wait_send()
        for copy in relays:
            copy.wait()


class ExpertSum:
    def __init__(self, r, sender, local, xyz, core):
        self.r, self.sender, self.core = r, sender, core
        self.plus, self.minus = ring_devices(xyz, core, 0, (1, 3))
        self.grads, self.near, self.passing = r.grads_in, r.near, r.passing
        self.quarter = [shifted(xyz, 0, by)[0] for by in range(4)]
        self.loads = [
            local.start(self.half(1, 0), r.mine.at[pl.ds(0, 3)]),
            local.start(self.half(3, 1), r.mine.at[pl.ds(3, 3)]),
            local.start(self.grads.at[self.quarter[0]], r.mine.at[pl.ds(6, 6)]),
        ]

    def half(self, by, half):
        return self.grads.at[self.quarter[by], pl.ds(3 * half, 3)]

    def near_half(self, side, half):
        return self.near.at[side, pl.ds(3 * half, 3)]

    def start(self):
        go = self.sender.start
        self.far = [
            go(self.half(2, 0), self.passing.at[0], self.plus),
            go(self.half(2, 1), self.passing.at[1], self.minus),
        ]
        self.plain = [
            go(self.half(1, 1), self.near_half(0, 1), self.plus),
            go(self.half(3, 0), self.near_half(1, 0), self.minus),
        ]

    def relay(self):
        for side, target in enumerate((self.plus, self.minus)):
            self.loads[side].wait()
            self.far[side].wait_recv()
            for i in range(3):
                own = self.r.mine[3 * side + i].astype(F32)
                self.passing[side, i] = (own + self.passing[side, i].astype(F32)).astype(BF)
            self.plain.append(
                self.sender.start(self.passing.at[side], self.near_half(side, side), target)
            )

    def finish(self):
        r = self.r
        self.loads[2].wait()
        for copy in self.plain:
            copy.wait()
        for copy in self.far:
            copy.wait_send()
        for i in (3, 4, 5, 0, 1, 2):
            value = r.mine[6 + i].astype(F32) + r.near[0, i].astype(F32) + r.near[1, i].astype(F32)
            if i >= 3:
                r.ship[i - 3] = value.astype(BF)
            else:
                r.total[self.core, i] = value.astype(BF)
            if i == 5:
                copy = self.sender.start(r.ship, r.total.at[self.core], partner())
        copy.wait()


EXPERT_SUM = dict(
    near=pltpu.VMEM((2, 6, HIDDEN, HIDDEN), BF),
    passing=pltpu.VMEM((2, 3, HIDDEN, HIDDEN), BF),
    mine=pltpu.VMEM((12, HIDDEN, HIDDEN), BF),
    ship=pltpu.VMEM((3, HIDDEN, HIDDEN), BF),
)


def tables(r):
    first = r.lengths[0, 0]
    second = first + r.lengths[0, 1]

    def place(index):
        segment = jnp.where(index >= first, 1, 0) + jnp.where(index >= second, 1, 0)
        start = jnp.where(segment == 0, 0, jnp.where(segment == 1, first, second))
        return segment, index - start

    shape = (TOKENS, TOKENS)
    lane = lax.broadcasted_iota(jnp.int32, shape, 1)
    row_segment, row_place = place(lax.broadcasted_iota(jnp.int32, shape, 0))
    key_segment, key_place = place(lane)
    allowed = (row_segment == key_segment) & (key_place <= row_place)
    r.allow[...] = jnp.where(allowed, 1.0, 0.0)
    half = jnp.where(lane < HEAD // 2, lane, lane - HEAD // 2).astype(F32)
    frequency = jnp.exp(half * (-2.0 / HEAD * math.log(rope_base)))
    angles = row_place.astype(F32) * frequency
    sign = jnp.where(lane < HEAD // 2, -1.0, 1.0)
    r.cos[...] = jnp.cos(angles)
    r.sin[...] = jnp.sin(angles) * sign


def assemble(r):
    square = (SHARD, SHARD)
    eye = lax.broadcasted_iota(jnp.int32, square, 0) == lax.broadcasted_iota(jnp.int32, square, 1)
    lane = lax.broadcasted_iota(jnp.int32, (SHARD, 128), 1)
    for l in range(LAYERS):
        r.shard[l, :, 0:768] = r.query[l]
        r.shard[l, :, 768:896] = r.key[l]
        r.shard[l, :, 896:QKV] = r.value[l]
        turned = dot(jnp.where(eye, 1.0, 0.0).astype(BF), r.out[l], 1, 1)
        r.shard[l, :, QKV : QKV + OUT] = turned.astype(BF)
        column = jnp.zeros((SHARD, 128), F32)
        for i, gain in enumerate((r.gain_a, r.gain_e)):
            spread = jnp.broadcast_to(gain[l : l + 1, :].astype(F32), square)
            spread = jnp.where(eye, spread, 0.0).astype(BF)
            column = column + dot(spread, jnp.where(lane == i, 1.0, 0.0).astype(BF))
        r.shard[l, :, QKV + OUT :] = column.astype(BF)


def gather_body(r):
    xyz, core = coords(), lax.axis_index("blk")
    count = hail([d for axis in range(3) for d in ring_devices(xyz, core, axis)] + [partner()])
    sender, local = Sender(r.send, r.recv), Local(r.local)
    mine = pl.ds(pl.multiple_of(core * HALF, HALF), HALF)
    here = [
        local.start(r.tok, r.tokens.at[:, mine]),
        local.start(r.cot_half, r.cot.at[:, mine]),
    ]
    assemble(r)
    for l, whole in enumerate((r.w0, r.w1)):
        here.append(local.start(r.shard.at[l], whole.at[xyz[0], xyz[1], xyz[2]]))
    heard(count)
    gather = Gather(sender, xyz, core)
    now = [(r.w0, p * PART, PART, order) for p, order in enumerate(ORDERS)]
    later = [(r.w1, *job) for job in LATER]
    first = [c for job in now for c in gather.first(job, r.shard.at[0])]
    first_later = [c for job in later for c in gather.first(job, r.shard.at[1])]
    others = [
        sender.start(r.tok, r.tokens.at[:, mine], partner()),
        sender.start(r.cot_half, r.cot.at[:, mine], partner()),
    ]
    for l in range(LAYERS):
        for name in ("gate", "up", "down"):
            ref = getattr(r, name).at[l, 1 - core]
            others.append(sender.start(ref, getattr(r, name + "_other").at[l], partner()))
    tables(r)
    for copy in here + first:
        copy.wait()
    near = [gather.near(job, 1) for job in now]
    for copy in first_later:
        copy.wait()
    near_later = [gather.near(job, 1) for job in later]
    relays = [gather.relay(job, 1, n) for job, n in zip(now, near)]
    relays_later = [gather.relay(job, 1, n) for job, n in zip(later, near_later)]
    for n, relay in zip(near, relays):
        gather.finish(n, relay)
    near = [gather.near(job, 2) for job in now]
    for n, relay in zip(near_later, relays_later):
        gather.finish(n, relay)
    relays = [gather.relay(job, 2, n) for job, n in zip(now, near)]
    for n, relay in zip(near, relays):
        gather.finish(n, relay)
    for copy in others:
        copy.wait()


KEPT = dict(
    h=((TOKENS, WIDE), F32),
    n=((TOKENS, WIDE), BF),
    qkv=((TOKENS, QKV), BF),
    prob=((HEADS, TOKENS, TOKENS), F32),
    o=((TOKENS, OUT), BF),
    onehot=((SLOTS, TOKENS), BF),
    weighted=((SLOTS, TOKENS), F32),
)
KEPT_SPACE = {name: pltpu.VMEM(*spec) for name, spec in KEPT.items()}
HELD = dict(
    held_gate=pltpu.VMEM((2, WIDE, HIDDEN), BF),
    held_up=pltpu.VMEM((2, WIDE, HIDDEN), BF),
    held_down=pltpu.VMEM((2, HIDDEN, WIDE), BF),
)
ROWS = ((SLOTS, WIDE), BF)
INNER = ((2, SLOTS, HIDDEN), F32)
BLOCKS = ((PEERS, CAP, WIDE), BF)
PLANE = ((TOKENS, WIDE), F32)
GRADS = ((4, 6, HIDDEN, HIDDEN), BF)
BACKWARD = dict(
    z=pltpu.VMEM((SLOTS, 2 * HIDDEN), BF),
    d=pltpu.VMEM((SLOTS, 4 * HIDDEN), BF),
    dy=pltpu.VMEM(*ROWS),
    stage=pltpu.VMEM((2, 6, HIDDEN, HIDDEN), BF),
)


def sems(**counts):
    return {name: pltpu.SemaphoreType.DMA((n,)) for name, n in counts.items()}


def spaces(**specs):
    return {name: pltpu.VMEM(*spec) for name, spec in specs.items()}


def front(r, x, pair, local):
    gain_a, gain_e = gain_rows(r.w)
    r.part0[...] = attention(
        x, gain_a, r.w, r.cos[...], r.sin[...], r.allow[...], r.n, r.qkv, r.prob, r.o
    )
    copy = pair.start(r.part0, r.theirs0, partner())
    for name in ("n", "qkv", "prob", "o", "onehot", "weighted"):
        local.keep(getattr(r, name), getattr(r, name + "_out"))
    copy.wait()
    h = x + (r.part0[...] + r.theirs0[...])
    r.h[...] = h
    local.keep(r.h, r.h_out)
    return (h * inverse_norm(h) * gain_e).astype(BF)


def forward_body(layer, r):
    xyz, core = coords(), lax.axis_index("blk")
    local, pair = Local(r.local), Sender(r.pair_send, r.pair_recv)
    load = local.start(r.w_any, r.w)
    count = hail(peers() + ring_devices(xyz, core, 0, (1, 3)))
    loads = expert_weight_copies(layer, r, local)
    hot, heavy = slot_matrices(r.ids[layer], r.weights[layer])
    r.onehot[...] = hot.astype(BF)
    r.weighted[...] = heavy
    heard(count)
    gather = Gather(Sender(r.wide_send, r.wide_recv), xyz, core)
    jobs = [(r.w1, *job) for job in LATER]
    near = [gather.near(job, 2) for job in jobs]
    load.wait()
    m = front(r, r.x[...].astype(F32), pair, local)
    store_rows(r.sent, dot(r.onehot[...], m))
    relays = {i: gather.relay(jobs[i], 2, near[i]) for i in (2, 3)}
    exchange_start(r.sent, r.came, r.send0, r.recv0)
    for copy in loads:
        copy.wait()
    exchange_wait(r.sent, r.came, r.send0, r.recv0)
    relays[0] = gather.relay(jobs[0], 2, near[0])
    r.rows[...] = rows_of(r.came)
    local.keep(r.rows, r.rows_out)
    held = (r.held_gate, r.held_up, r.held_down)
    store_rows(r.sent, expert_forward(r.rows[...], held, r.a, r.b))
    exchange_start(r.sent, r.back, r.send1, r.recv1)
    relays[1] = gather.relay(jobs[1], 2, near[1])
    local.keep(r.a, r.a_out)
    local.keep(r.b, r.b_out)
    exchange_wait(r.sent, r.back, r.send1, r.recv1)
    r.part1[...] = combine(r.weighted[...], rows_of(r.back))
    pair.start(r.part1, r.theirs1, partner()).wait()
    r.stream[...] = r.h[...] + (r.part1[...] + r.theirs1[...])
    for i in range(4):
        gather.finish(near[i], relays[i])
    local.wait_kept()


def middle_body(layer, r):
    local, pair = Local(r.local), Sender(r.pair_send, r.pair_recv)
    load = local.start(r.w_any, r.w)
    count = hail(peers())
    loads = expert_weight_copies(layer, r, local)
    hot, heavy = slot_matrices(r.ids[layer], r.weights[layer])
    r.onehot[...] = hot.astype(BF)
    r.weighted[...] = heavy
    slot_weight = jnp.sum(heavy, axis=1, keepdims=True)
    store_rows(r.sent_g, dot(r.onehot[...], r.cot[...]) * slot_weight)
    heard(count)
    exchange_start(r.sent_g, r.came_g, r.send1, r.recv1)
    load.wait()
    m = front(r, r.x[...], pair, local)
    store_rows(r.sent, dot(r.onehot[...], m))
    exchange_wait(r.sent_g, r.came_g, r.send1, r.recv1)
    exchange_start(r.sent, r.came, r.send0, r.recv0)
    r.dy[...] = rows_of(r.came_g)
    for copy in loads:
        copy.wait()
    exchange_wait(r.sent, r.came, r.send0, r.recv0)
    r.rows[...] = rows_of(r.came)
    held = (r.held_gate, r.held_up, r.held_down)
    store_rows(r.sent, expert_forward(r.rows[...], held, r.a, r.b))
    exchange_start(r.sent, r.y_back, r.send2, r.recv2)
    store_rows(r.turn, expert_backward(r.dy[...], held, r.a, r.b, r.z, r.d))
    local.keep(r.turn, r.m_back)
    local.kept += expert_gradients(r.rows, r.dy, r.z, r.d, r.stage, r.grads, local)
    exchange_wait(r.sent, r.y_back, r.send2, r.recv2)
    local.wait_kept()


def turned(value):
    return value.astype(F32).T.reshape(4, 4, 4, SHARD, TOKENS).astype(BF)


def own_part(ref, axis, index):
    return ref.at[:, index] if axis == 1 else ref.at[:, :, index]


def share_factor(ref, into, axis, sender, xyz, core):
    copies = []
    for by in (1, 3, 2):
        there = shifted(xyz, axis, by)
        copies.append(
            sender.start(own_part(ref, axis, there[axis]), into.at[by - 1], device_at(there, core))
        )
    return copies


def share_whole(ref, into, axis, sender, xyz, core):
    return [
        sender.start(ref, into.at[pl.ds(by * TOKENS, TOKENS)], device_at(shifted(xyz, axis, by), core))
        for by in (1, 3, 2)
    ]


def quarter_sum(own, came, axis, xyz, right):
    first = own_part(own, axis, xyz[axis])[...]
    pieces = [first] + [came[i] for i in range(3)]
    left = [p.astype(F32).reshape(HIDDEN, TOKENS).astype(BF) for p in pieces]
    return dot(jnp.concatenate(left, axis=1), right[...])


def back_body(last, r):
    xyz, core = coords(), lax.axis_index("blk")
    local, pair = Local(r.local), Sender(r.pair_send, r.pair_recv)
    sender = Sender(r.wide_send, r.wide_recv)
    load = local.start(r.w_any, r.w)
    count = hail(peers() + ring_devices(xyz, core, 0, (1, 3) if last else (1, 2, 3)))
    expert_sum = ExpertSum(r, sender, local, xyz, core)
    heard(count)
    exchange_start(r.m_came, r.came, r.send0, r.recv0)
    expert_sum.start()
    if last:
        loads = expert_weight_copies(0, r, local)
    r.n_turned[...] = turned(r.n[...])
    if not last:
        r.sum_a[1] = r.sum_a_in[...]
        r.sum_b[1] = r.sum_b_in[...]
    r.o_all[0:TOKENS] = r.o[...]
    load.wait()
    gain_a, gain_e = gain_rows(r.w)
    if not last:
        old = late_start(r, 1, sender, xyz, core)
    exchange_wait(r.m_came, r.came, r.send0, r.recv0)
    r.part0[...] = dot(r.onehot[...], rows_of(r.came), 0, 0)
    copy = pair.start(r.part0, r.theirs0, partner())
    shared = share_factor(r.n_turned, r.n_came, 1, sender, xyz, core)
    shared += share_whole(r.o, r.o_all, 2, sender, xyz, core)
    if not last:
        old = late_middle(r, 1, sender, xyz, core, old)
    copy.wait()
    dm = r.part0[...] + r.theirs0[...]
    hidden = r.h[...]
    inward, gain_grad_e = norm_back(hidden, inverse_norm(hidden), gain_e, dm)
    gh = r.upstream[...].astype(F32) + inward
    r.flow[...] = gh
    da = gh.astype(BF)
    r.da_turned[...] = turned(gh)
    shared += share_factor(r.da_turned, r.da_came, 2, sender, xyz, core)
    do = dot(da, r.w[:, QKV : QKV + OUT]).astype(BF)
    key = r.qkv[:, HEADS * HEAD : (HEADS + 1) * HEAD]
    value = r.qkv[:, (HEADS + 1) * HEAD :]
    scale = HEAD ** (-0.5)
    key_grad, value_grad = None, None
    cosine, sine = r.cos[...], r.sin[...]
    lin = r.lin_all
    for i in range(HEADS):
        prob_i = r.prob[i]
        do_i = head_of(do, i)
        q_i = r.qkv[:, i * HEAD : (i + 1) * HEAD]
        dprob = dot(do_i, value, 1, 1)
        centre = jnp.sum(prob_i * dprob, axis=-1, keepdims=True)
        ds = (prob_i * (dprob - centre)).astype(BF)
        dq = dot(ds, key) * scale
        lin[0:TOKENS, i * HEAD : (i + 1) * HEAD] = unrotate(dq, cosine, sine).astype(BF)
        dk = dot(ds, q_i, 0, 0)
        dv = dot(prob_i.astype(BF), do_i, 0, 0)
        key_grad = dk if key_grad is None else key_grad + dk
        value_grad = dv if value_grad is None else value_grad + dv
    lin[0:TOKENS, HEADS * HEAD : (HEADS + 1) * HEAD] = unrotate(
        key_grad * scale, cosine, sine
    ).astype(BF)
    lin[0:TOKENS, (HEADS + 1) * HEAD :] = value_grad.astype(BF)
    r.part1[...] = dot(lin[0:TOKENS, :], r.w[:, 0:QKV], 1, 1)
    across = pair.start(r.part1, r.theirs1, partner())
    if not last:
        shared += share_whole(lin.at[pl.ds(0, TOKENS)], lin, 1, sender, xyz, core)
        expert_sum.relay()
    across.wait()
    dn = r.part1[...] + r.theirs1[...]
    x = r.x[...].astype(F32)
    inward, gain_grad_a = norm_back(x, inverse_norm(x), gain_a, dn)
    flow = r.flow[...] + inward
    row = lax.broadcasted_iota(jnp.int32, (8, WIDE), 0)
    gains = jnp.zeros((8, WIDE), F32)
    for i, grad in enumerate((gain_grad_a, gain_grad_e)):
        grad = jnp.sum(grad, axis=0, keepdims=True)
        gains = jnp.where(row == i + (2 if last else 0), jnp.broadcast_to(grad, (8, WIDE)), gains)
    if not last:
        r.tokens_grad[...] = jnp.where(core == 1, flow[:, HALF:], flow[:, :HALF])
        finish_sums(r, shared, gains + r.gains_in[...], old, expert_sum, sender, xyz, core)
        return
    r.gains[...] = gains
    r.flow[...] = flow
    slot_weight = jnp.sum(r.weighted_next[...], axis=1, keepdims=True)
    high, low = halves(flow)
    hot = r.onehot_next[...]
    store_rows(r.sent, (dot(hot, high) + dot(hot, low)) * slot_weight)
    exchange_start(r.sent, r.came_g, r.send1, r.recv1)
    local.keep(r.flow, r.flow_out)
    expert_sum.relay()
    shared += share_whole(lin.at[pl.ds(0, TOKENS)], lin, 1, sender, xyz, core)
    mixed = combine(r.weighted[...], rows_of(r.y_back))
    r.half[...] = jnp.where(core == 1, mixed[:, :HALF], mixed[:, HALF:])
    copy = pair.start(r.half, r.half_theirs, partner())
    own = jnp.where(core == 1, mixed[:, HALF:], mixed[:, :HALF])
    kept = jnp.where(core == 1, r.h[:, HALF:], r.h[:, :HALF])
    copy.wait()
    r.block_out[...] = (kept + (own + r.half_theirs[...])).astype(BF)
    for copy in loads:
        copy.wait()
    exchange_wait(r.sent, r.came_g, r.send1, r.recv1)
    r.dy[...] = rows_of(r.came_g)
    held = (r.held_gate, r.held_up, r.held_down)
    store_rows(r.turn, expert_backward(r.dy[...], held, r.a, r.b, r.z, r.d))
    local.keep(r.turn, r.m_back)
    local.kept += expert_gradients(r.rows, r.dy, r.z, r.d, r.stage, r.grads, local)
    for copy in shared:
        copy.wait()
    wide = (4, 4, SHARD, QKV)
    r.sum_a[...] = quarter_sum(r.n_turned, r.n_came, 1, xyz, lin).reshape(wide).astype(BF)
    wide = (4, 4, SHARD, OUT)
    r.sum_b[...] = quarter_sum(r.da_turned, r.da_came, 2, xyz, r.o_all).reshape(wide).astype(BF)
    expert_sum.finish()
    local.wait_kept()


def late_start(r, l, sender, xyz, core):
    copies = []
    for ref, came, axis in ((r.sum_a, r.near_a, 2), (r.sum_b, r.near_b, 1)):
        for by in (1, 3, 2):
            there = shifted(xyz, axis, by)
            copies.append(
                sender.start(ref.at[l, :, there[axis]], came.at[l, by - 1], device_at(there, core))
            )
    return copies


def late_middle(r, l, sender, xyz, core, copies):
    for copy in copies:
        copy.wait()
    for ref, came, axis, lanes in (
        (r.sum_a, r.near_a, 2, slice(0, QKV)),
        (r.sum_b, r.near_b, 1, slice(QKV, QKV + OUT)),
    ):
        total = ref[l, :, xyz[axis]].astype(F32)
        for i in range(3):
            total = total + came[l, i].astype(F32)
        r.line[l, :, :, lanes] = total.astype(BF)
    copies = []
    for by in (1, 3, 2):
        there = shifted(xyz, 0, by)
        copies.append(
            sender.start(r.line.at[l, there[0]], r.line_came.at[l, by - 1], device_at(there, core))
        )
    return copies


def late_end(r, l, xyz, copies):
    for copy in copies:
        copy.wait()
    total = r.line[l, xyz[0]].astype(F32)
    for i in range(3):
        total = total + r.line_came[l, i].astype(F32)
    r.weight_grad[l] = total


def gains_along(r, axis, sender, xyz, core):
    return [
        sender.start(r.gain_sum.at[axis], r.gain_came.at[axis, by - 1], device_at(shifted(xyz, axis, by), core))
        for by in (1, 3, 2)
    ]


def gains_next(r, axis, copies):
    for copy in copies:
        copy.wait()
    total = r.gain_sum[axis]
    for i in range(3):
        total = total + r.gain_came[axis, i]
    return total


def finish_sums(r, shared, gains, old, expert_sum, sender, xyz, core):
    r.gain_sum[1] = gains
    along = gains_along(r, 1, sender, xyz, core)
    for copy in shared:
        copy.wait()
    wide = (4, 4, SHARD, QKV)
    r.sum_a[0] = quarter_sum(r.n_turned, r.n_came, 1, xyz, r.lin_all).reshape(wide).astype(BF)
    wide = (4, 4, SHARD, OUT)
    r.sum_b[0] = quarter_sum(r.da_turned, r.da_came, 2, xyz, r.o_all).reshape(wide).astype(BF)
    new = late_start(r, 0, sender, xyz, core)
    r.gain_sum[2] = gains_next(r, 1, along)
    along = gains_along(r, 2, sender, xyz, core)
    late_end(r, 1, xyz, old)
    new = late_middle(r, 0, sender, xyz, core, new)
    r.gain_sum[0] = gains_next(r, 2, along)
    along = gains_along(r, 0, sender, xyz, core)
    late_end(r, 0, xyz, new)
    r.gain_total[...] = gains_next(r, 0, along)
    expert_sum.finish()


def kernel_call(body, name, cid, ins, outs, scratch, aliases=()):
    names = [*ins, *outs, *scratch]
    assert len(set(names)) == len(names)

    def kernel(*refs):
        body(types.SimpleNamespace(**dict(zip(names, refs))))

    results = pl.pallas_call(
        kernel,
        out_shape=[jax.ShapeDtypeStruct(shape, kind) for shape, kind, _ in outs.values()],
        in_specs=[space for _, space in ins.values()],
        out_specs=[space for _, _, space in outs.values()],
        scratch_shapes=list(scratch.values()),
        input_output_aliases={list(ins).index(a): list(outs).index(b) for a, b in aliases},
        compiler_params=pltpu.CompilerParams(
            collective_id=cid, has_side_effects=True, vmem_limit_bytes=LIMIT
        ),
        name=name,
    )(*[array for array, _ in ins.values()])
    return types.SimpleNamespace(**dict(zip(outs, results)))


def per_device(
    tokens_in,
    seq_lengths,
    expert_ids,
    gate_weights,
    attention_gain,
    query_weight,
    key_weight,
    value_weight,
    out_weight,
    expert_gain,
    gate_weight,
    up_weight,
    down_weight,
    cotangent,
):
    cube = (4, 4, 4, SHARD, COLS)
    own = dict(gate=(gate_weight, ANY), up=(up_weight, ANY), down=(down_weight, ANY))
    start = kernel_call(
        gather_body,
        "gather",
        1,
        dict(
            lengths=(seq_lengths, SMEM),
            query=(query_weight, VMEM),
            key=(key_weight, VMEM),
            value=(value_weight, VMEM),
            out=(out_weight, VMEM),
            gain_a=(attention_gain, VMEM),
            gain_e=(expert_gain, VMEM),
            tok=(tokens_in, VMEM),
            cot_half=(cotangent, VMEM),
            **own,
        ),
        dict(
            w0=(cube, BF, ANY),
            w1=(cube, BF, ANY),
            tokens=((TOKENS, WIDE), BF, VMEM),
            cot=((TOKENS, WIDE), BF, VMEM),
            cos=((TOKENS, HEAD), F32, VMEM),
            sin=((TOKENS, HEAD), F32, VMEM),
            allow=((TOKENS, TOKENS), F32, VMEM),
            gate_other=((LAYERS, WIDE, HIDDEN), BF, ANY),
            up_other=((LAYERS, WIDE, HIDDEN), BF, ANY),
            down_other=((LAYERS, HIDDEN, WIDE), BF, ANY),
        ),
        dict(
            shard=pltpu.VMEM((LAYERS, SHARD, COLS), BF),
            **sems(send=72, recv=72, local=4),
        ),
    )
    experts = dict(
        own,
        gate_other=(start.gate_other, ANY),
        up_other=(start.up_other, ANY),
        down_other=(start.down_other, ANY),
    )
    trig = dict(cos=(start.cos, VMEM), sin=(start.sin, VMEM))
    routing = dict(ids=(expert_ids, VMEM), weights=(gate_weights, VMEM))
    kept_out = {name + "_out": (*spec, ANY) for name, spec in KEPT.items()}
    w_space = dict(w=pltpu.VMEM((WIDE, COLS), BF))
    exchanges = sems(send0=PEERS, recv0=PEERS, send1=PEERS, recv1=PEERS, pair_send=4, pair_recv=4)
    w0 = start.w0.reshape(WIDE, COLS)
    below = kernel_call(
        functools.partial(forward_body, 0),
        "forward",
        2,
        dict(
            x=(start.tokens, VMEM),
            w_any=(w0, ANY),
            w1_in=(start.w1, ANY),
            allow=(start.allow, VMEM),
            **trig,
            **routing,
            **experts,
        ),
        dict(
            w1=(cube, BF, ANY),
            stream=(*PLANE, VMEM),
            rows_out=(*ROWS, ANY),
            a_out=(*INNER, ANY),
            b_out=(*INNER, ANY),
            **kept_out,
        ),
        dict(
            **w_space,
            **KEPT_SPACE,
            **HELD,
            **spaces(sent=BLOCKS, came=BLOCKS, back=BLOCKS, rows=ROWS, a=INNER, b=INNER),
            **spaces(part0=PLANE, theirs0=PLANE, part1=PLANE, theirs1=PLANE),
            **exchanges,
            **sems(wide_send=16, wide_recv=16, local=20),
        ),
        [("w1_in", "w1")],
    )
    w1 = below.w1.reshape(WIDE, COLS)
    above = kernel_call(
        functools.partial(middle_body, 1),
        "middle",
        3,
        dict(
            x=(below.stream, VMEM),
            cot=(start.cot, VMEM),
            w_any=(w1, ANY),
            allow=(start.allow, VMEM),
            **trig,
            **routing,
            **experts,
        ),
        dict(
            y_back=(*BLOCKS, ANY),
            m_back=(*BLOCKS, ANY),
            grads=(*GRADS, ANY),
            **kept_out,
        ),
        dict(
            **w_space,
            **KEPT_SPACE,
            **HELD,
            **spaces(sent=BLOCKS, came=BLOCKS, sent_g=BLOCKS, came_g=BLOCKS, turn=BLOCKS),
            **spaces(rows=ROWS, a=INNER, b=INNER, part0=PLANE, theirs0=PLANE),
            **BACKWARD,
            **exchanges,
            **sems(send2=PEERS, recv2=PEERS, local=20),
        ),
    )

    def kept(of):
        return {name: (getattr(of, name + "_out"), VMEM) for name in KEPT}

    total = ((2, 3, HIDDEN, HIDDEN), BF, VMEM)
    part_a, part_b = (4, 4, SHARD, QKV), (4, 4, SHARD, OUT)
    back_space = dict(
        **w_space,
        **EXPERT_SUM,
        **spaces(came=BLOCKS, part0=PLANE, theirs0=PLANE, part1=PLANE, theirs1=PLANE, flow=PLANE),
        n_turned=pltpu.VMEM((4, 4, 4, SHARD, TOKENS), BF),
        da_turned=pltpu.VMEM((4, 4, 4, SHARD, TOKENS), BF),
        n_came=pltpu.VMEM((3, 4, 4, SHARD, TOKENS), BF),
        da_came=pltpu.VMEM((3, 4, 4, SHARD, TOKENS), BF),
        lin_all=pltpu.VMEM((4 * TOKENS, QKV), BF),
        o_all=pltpu.VMEM((4 * TOKENS, OUT), BF),
        **exchanges,
        **sems(local=20),
    )
    turn = kernel_call(
        functools.partial(back_body, True),
        "back_above",
        4,
        dict(
            x=(below.stream, VMEM),
            upstream=(start.cot, VMEM),
            w_any=(w1, ANY),
            **trig,
            **kept(above),
            m_came=(above.m_back, ANY),
            y_back=(above.y_back, VMEM),
            grads_in=(above.grads, ANY),
            onehot_next=(below.onehot_out, VMEM),
            weighted_next=(below.weighted_out, VMEM),
            rows=(below.rows_out, VMEM),
            a=(below.a_out, VMEM),
            b=(below.b_out, VMEM),
            **experts,
        ),
        dict(
            flow_out=(*PLANE, ANY),
            m_back=(*BLOCKS, ANY),
            grads=(*GRADS, ANY),
            block_out=((TOKENS, HALF), BF, VMEM),
            total=total,
            gains=((8, WIDE), F32, VMEM),
            sum_a=(part_a, BF, VMEM),
            sum_b=(part_b, BF, VMEM),
        ),
        dict(
            **back_space,
            **HELD,
            **BACKWARD,
            **spaces(sent=BLOCKS, came_g=BLOCKS, turn=BLOCKS),
            half=pltpu.VMEM((TOKENS, HALF), F32),
            half_theirs=pltpu.VMEM((TOKENS, HALF), F32),
            **sems(wide_send=24, wide_recv=24),
        ),
    )
    end = kernel_call(
        functools.partial(back_body, False),
        "back_below",
        5,
        dict(
            x=(start.tokens, VMEM),
            upstream=(turn.flow_out, VMEM),
            w_any=(w0, ANY),
            **trig,
            **kept(below),
            m_came=(turn.m_back, ANY),
            grads_in=(turn.grads, ANY),
            gains_in=(turn.gains, VMEM),
            sum_a_in=(turn.sum_a, VMEM),
            sum_b_in=(turn.sum_b, VMEM),
        ),
        dict(
            tokens_grad=((TOKENS, HALF), F32, VMEM),
            total=total,
            weight_grad=((LAYERS, SHARD, QKV + OUT), F32, VMEM),
            gain_total=((8, WIDE), F32, VMEM),
        ),
        dict(
            **back_space,
            sum_a=pltpu.VMEM((LAYERS, *part_a), BF),
            sum_b=pltpu.VMEM((LAYERS, *part_b), BF),
            near_a=pltpu.VMEM((LAYERS, 3, 4, SHARD, QKV), BF),
            near_b=pltpu.VMEM((LAYERS, 3, 4, SHARD, OUT), BF),
            line=pltpu.VMEM((LAYERS, 4, SHARD, QKV + OUT), BF),
            line_came=pltpu.VMEM((LAYERS, 3, SHARD, QKV + OUT), BF),
            gain_sum=pltpu.VMEM((3, 8, WIDE), F32),
            gain_came=pltpu.VMEM((3, 3, 8, WIDE), F32),
            **sems(wide_send=48, wide_recv=48),
        ),
    )
    place = (lax.axis_index("dp") * PEERS + lax.axis_index("expert")) * SHARD
    gains = lax.dynamic_slice_in_dim(end.gain_total, place, SHARD, 1)
    att = end.weight_grad
    both = [jnp.stack([end.total[:, i], turn.total[:, i]]).astype(F32) for i in range(3)]
    return (
        turn.block_out,
        end.tokens_grad,
        gains[0:4:2],
        att[:, :, :768],
        att[:, :, 768:896],
        att[:, :, 896:QKV],
        jnp.swapaxes(att[:, :, QKV:], 1, 2),
        gains[1:4:2],
        *both,
    )


def solution(mesh):
    placed = (
        P(("dp", "expert"), "blk"),
        P(("dp", "expert"), None),
        P(None, ("dp", "expert"), None),
        P(None, ("dp", "expert"), None),
        P(None, ("dp", "expert")),
        P(None, ("dp", "expert"), "blk"),
        P(None, ("dp", "expert"), "blk"),
        P(None, ("dp", "expert"), "blk"),
        P(None, "blk", ("dp", "expert")),
        P(None, ("dp", "expert")),
        P(None, "expert", None, "blk"),
        P(None, "expert", None, "blk"),
        P(None, "expert", "blk", None),
        P(("dp", "expert"), "blk"),
    )
    return jax.shard_map(
        per_device,
        mesh=mesh,
        in_specs=placed,
        out_specs=(
            P(("dp", "expert"), "blk"),
            P(("dp", "expert"), "blk"),
            P(None, ("dp", "expert")),
            P(None, ("dp", "expert"), "blk"),
            P(None, ("dp", "expert"), "blk"),
            P(None, ("dp", "expert"), "blk"),
            P(None, "blk", ("dp", "expert")),
            P(None, ("dp", "expert")),
            P(None, "expert", "dp", "blk"),
            P(None, "expert", "dp", "blk"),
            P(None, "expert", "blk", "dp"),
        ),
        check_vma=False,
    )
```

time: 510 us -> 345 us (0.68)
  waiting for transfers between devices: 75.9 us -> 0 us
  Pallas kernels: 382 us -> 325 us
  between operations: 14.5 us -> 0.94 us
  other arithmetic: 13.9 us -> 4.05 us
    reduce_scatter x2 -> x0, waiting for transfers between devices: 73.3 us -> none  [summed(): total = lax.psum_scatter(grads, 'dp', scatter_dimension=0, tiled=True)[0]]
    pallas_call x7 -> x5, Pallas kernels: 382 us -> 325 us  [kernel_call(): pl.pallas_call(kernel, out_shape=[jax.ShapeDtypeStruct(shape, kind) for s...]
    another operation x11 -> x0, other arithmetic: 7.51 us -> none  [the longest x9 5.18 us: per_device(): jnp.stack([first, second])]
  transfers between devices with their start and end apart: 4 -> 0, of which waited for: 2 -> 0; matrix products, arithmetic and copies ran while one was open for 2% -> 0% of each run, Pallas kernels for 25% -> 0%
where the time goes in v2:
time: 345 us; the launch traced here: 340 us
  Pallas kernels  325 us (94%)
  local copies, waits for them, and re-layouts  10.3 us (3%)
  other arithmetic  4.05 us (1%)
    pallas_call x5, Pallas kernels, kernel_call(): pl.pallas_call(kernel, out_shape=[jax.ShapeDtypeStruct(shape, kind) for s...  325 us

profile of v2, /device:TPU:0, one launch (start us, length us, event | category | flops | bytes accessed | tf_op | source)
XLA Modules:
  0.0 340.1 jit_solution(5022589359273924343)
XLA Ops:
  0.6 1.8 copy.26.refs_4_
  2.4 0.0 copy-start.4
  2.5 0.0 copy-start.5
  2.5 44.6 %gather.1 = (bf16[4,4,4,24,1920]{4,3,2,1,0:T(8,128)(2,1)}, bf16[4,4,4,24,1920]{4,3,2,1,0:T(8,128)(2,1)}, bf16[128,1536]{1,0:T(8,128)(2,1)}, bf16[128,1536]{1,0:T...) custom-call(s32[1,3]{1,0:T(1,128)} %refs_0_.1, ...), custom_call_target="tpu_custom_call" | custom-call | tf_op jit(solution)/shard_map/gather/pallas_call | solution.py:867
  47.0 0.0 copy-done.4
  47.0 0.8 copy.27.refs_6_
  47.8 0.0 copy-done.5
  47.8 0.8 copy.28.refs_7_
  48.6 55.6 %forward.1 = (bf16[4,4,4,24,1920]{4,3,2,1,0:T(8,128)(2,1)}, f32[128,1536]{1,0:T(8,128)}, bf16[384,1536]{1,0:T(8,128)(2,1)}, f32[2,384,384]{2,1,0:T(8,128)}, f32[...) custom-call(bf16[128,1536]{1,0:T(8,128)(2,1)} %get-tuple-element.55., ...), custom_call_target="tpu_custom_call", output_to_operand_aliasing={{0}: (2, {})} | custom-call | tf_op jit(solution)/shard_map/forward/pallas_call | solution.py:867
  104.2 61.5 %middle.1 = (bf16[16,24,1536]{2,1,0:T(8,128)(2,1)}, bf16[16,24,1536]{2,1,0:T(8,128)(2,1)}, bf16[4,6,384,384]{3,2,1,0:T(8,128)(2,1)}, f32[128,1536]{1,0:T(8,128)}...) custom-call(f32[128,1536]{1,0:T(8,128)} %get-tuple-element.64.refs_0, ...), custom_call_target="tpu_custom_call" | custom-call | tf_op jit(solution)/shard_map/middle/pallas_call | solution.py:867
  165.7 76.2 %back_above.1 = (f32[128,1536]{1,0:T(8,128)}, bf16[16,24,1536]{2,1,0:T(8,128)(2,1)}, bf16[4,6,384,384]{3,2,1,0:T(8,128)(2,1)}, bf16[128,768]{1,0:T(8,128)(2,1)},...) custom-call(f32[128,1536]{1,0:T(8,128)} %get-tuple-element.64.refs_0, ...), custom_call_target="tpu_custom_call" | custom-call | tf_op jit(solution)/shard_map/back_above/pallas_call | solution.py:867
  242.0 86.9 %back_below.1 = (f32[128,768]{1,0:T(8,128)}, bf16[2,3,384,384]{3,2,1,0:T(8,128)(2,1)}, f32[2,24,1792]{2,1,0:T(8,128)}, f32[8,1536]{1,0:T(8,128)}) custom-call(bf16[128,1536]{1,0:T(8,128)(2,1)} %get-tuple-element.55.refs_0_, f32[128,1536]{1,0:T(8,128)} %get-tuple-element.83.refs_1_, bf16[1536,1920]{1,0:T(8,128)(2,1)} %bitcast.19, ...), custom_call_target="tpu_custom_call" | custom-call | tf_op jit(solution)/shard_map/back_below/pallas_call | solution.py:867
  328.9 0.0 copy-start
  328.9 1.7 slice_bitcast_fusion.3
  330.7 0.3 copy-done
  330.9 0.2 slice_bitcast_fusion
  331.1 1.6 maximum_convert_fusion.2
  332.7 0.0 copy-start.2
  332.7 0.0 copy-start.3
  332.7 0.0 copy-start.1
  332.7 2.5 maximum_convert_fusion
  335.2 0.0 copy-done.2
  335.2 0.7 slice_bitcast_fusion.6
  335.9 0.6 fusion
  336.5 0.8 constant_dynamic-slice_fusion
  337.3 0.6 slice.36
  337.9 0.6 slice.41
  338.4 0.0 copy-done.3
  338.5 0.7 copy.39
  339.1 0.0 copy-done.1
  339.1 0.7 copy.40
Async XLA Ops:
  2.4 44.6 %copy-start.4 = (s32[2,128,4]{1,2,0:T(4,128)S(1)}, s32[2,128,4]{1,2,0:T(4,128)}, u32[]{:S(2)}) copy-start(s32[2,128,4]{1,2,0:T(4,128)} %param.16) | copy-start | bytes 12292
  2.5 45.4 %copy-start.5 = (f32[2,128,4]{1,2,0:T(4,128)S(1)}, f32[2,128,4]{1,2,0:T(4,128)}, u32[]{:S(2)}) copy-start(f32[2,128,4]{1,2,0:T(4,128)} %param.17) | copy-start | bytes 12292
  328.9 2.0 copy-start
  332.7 2.5 copy-start.2
  332.7 5.8 %copy-start.3 = (bf16[128,768]{1,0:T(8,128)(2,1)S(1)}, bf16[128,768]{1,0:T(8,128)(2,1)}, u32[]{:S(2)}) copy-start(bf16[128,768]{1,0:T(8,128)(2,1)} %get-tuple-element.122) | copy-start | bytes 589828
  332.7 6.4 %copy-start.1 = (f32[128,768]{1,0:T(8,128)S(1)}, f32[128,768]{1,0:T(8,128)}, u32[]{:S(2)}) copy-start(f32[128,768]{1,0:T(8,128)} %get-tuple-element.123) | copy-start | bytes 1179652
